TPU v7x, 32 devices: a whole 2x2x4 slice. The times are simulated.
32 devices in a mesh: row: 8 (over z, y), col: 4 (over x, core).
Axes of the slice: x: 2, y: 2, z: 4, core: 2. Of those that a mesh axis runs over, the one named last changes fastest.
Arguments:
- object_field: float32 [2, 1024, 512], P(None, 'row', 'col'), may hold values from -5 to 5
- probe: float32 [2, 2, 256, 256], replicated, may hold values from -5 to 5
- amplitudes: float32 [8, 4, 2, 256, 256], P('row', 'col'), may hold values from 0.2 to 2.5
- offsets: int32 [8, 4, 2, 2], P('row', 'col'), may hold values from -128 to 0
Outputs:
- object_out: float32 [2, 1024, 512], P(None, 'row', 'col')
- probe_out: float32 [2, 2, 256, 256], replicated
Inputs may be any that keep to these rules, and one draw needn't show every extreme that they name: `offsets`: each scan's 256 x 256 window starts at this offset from its own tile's anchor, so it reaches at most 128 pixels into neighbouring tiles.
All inputs are finite; a program needn't handle non-finite values.
Results may differ from a plain program's by a relative error of at most 0.0003.
Values sent between devices are 32-bit elements; how exact they have to be, the bound alone decides.
A program may use at most 128 MiB of HBM per device.

v0:
```python
import math

import jax
import jax.numpy as jnp
import numpy as np
import ml_dtypes
from jax import lax
from jax.experimental import pallas as pl
from jax.experimental.pallas import tpu as pltpu
from jax.sharding import PartitionSpec as P

ITERS = 2
FLOOR = 0.5
OBJECT_STEP = 0.5
OBJECT_REG = 0.5
PROBE_STEP = 1.0
PROBE_REG = 1.0
F32 = jnp.float32
BF16 = jnp.bfloat16


def padded_2(cells, sides, width):
    for axis, dim in sides:
        count = lax.axis_size(axis)
        ends = count - 1
        head = lax.slice_in_dim(cells, 0, width, axis=dim)
        tail = lax.slice_in_dim(cells, cells.shape[dim] - width, cells.shape[dim], axis=dim)
        cells = jnp.concatenate(
            [
                lax.ppermute(tail, axis, [(i, (i + 1) % count) for i in range(ends)]),
                cells,
                lax.ppermute(head, axis, [((i + 1) % count, i) for i in range(ends)]),
            ],
            axis=dim,
        )
    return cells


def split_np(table):
    high = table.astype(np.float32).astype(ml_dtypes.bfloat16)
    low = (table - high.astype(np.float64)).astype(np.float32).astype(ml_dtypes.bfloat16)
    return [high, low]


def tables(side):
    half = side // 2
    n = np.arange(half)[:, None]
    k = np.arange(half)[None, :]
    pieces = []
    for odd in (0, 1):
        angle = 2.0 * math.pi * ((n * (2 * k + odd)) % side) / side
        cos, sin = np.cos(angle) / math.sqrt(side), np.sin(angle) / math.sqrt(side)
        forward = np.block([[cos, -sin], [sin, cos]])
        pieces += split_np(forward) + split_np(forward.T)
    return np.stack(pieces)


def order_table(side):
    half = side // 2
    place = np.concatenate([2 * np.arange(half), 2 * np.arange(half) + 1])
    table = np.zeros((side, side), np.float32)
    table[place, np.arange(side)] = 1.0
    return np.stack([table, table.T]).astype(ml_dtypes.bfloat16)


def split(x):
    high = x.astype(BF16)
    return high, (x - high.astype(F32)).astype(BF16)


def dot(a, b):
    return jnp.dot(a, b, preferred_element_type=F32)


def right(x, tab, at):
    high, low = split(x)
    return dot(high, tab[at]) + (dot(high, tab[at + 1]) + dot(low, tab[at]))


def left(tab, at, x):
    high, low = split(x)
    return dot(tab[at], high) + (dot(tab[at + 1], high) + dot(tab[at], low))


FE, GE, FO, GO = 0, 2, 4, 6


def forward(re, im, tab):
    h = re.shape[1] // 2
    even = right(jnp.concatenate([re[:, :h] + re[:, h:], im[:, :h] + im[:, h:]], 1), tab, FE)
    odd = right(jnp.concatenate([re[:, :h] - re[:, h:], im[:, :h] - im[:, h:]], 1), tab, FO)
    re = jnp.concatenate([even[:, :h], odd[:, :h]], 1)
    im = jnp.concatenate([even[:, h:], odd[:, h:]], 1)
    even = left(tab, GE, jnp.concatenate([re[:h] + re[h:], im[:h] + im[h:]], 0))
    odd = left(tab, GO, jnp.concatenate([re[:h] - re[h:], im[:h] - im[h:]], 0))
    return (
        jnp.concatenate([even[:h], odd[:h]], 0),
        jnp.concatenate([even[h:], odd[h:]], 0),
    )


def inverse(re, im, tab):
    h = re.shape[1] // 2
    even = left(tab, FE, jnp.concatenate([re[:h], im[:h]], 0))
    odd = left(tab, FO, jnp.concatenate([re[h:], im[h:]], 0))
    low, high = even + odd, even - odd
    re = jnp.concatenate([low[:h], high[:h]], 0)
    im = jnp.concatenate([low[h:], high[h:]], 0)
    even = right(jnp.concatenate([re[:, :h], im[:, :h]], 1), tab, GE)
    odd = right(jnp.concatenate([re[:, h:], im[:, h:]], 1), tab, GO)
    low, high = even + odd, even - odd
    return (
        jnp.concatenate([low[:, :h], high[:, :h]], 1),
        jnp.concatenate([low[:, h:], high[:, h:]], 1),
    )


def step_kernel(starts, obj, probe, amp, tab, order, grad, pgrad, wide):
    side = probe.shape[2]
    full = obj.shape[1]
    modes = probe.shape[1]
    scans = amp.shape[0]
    wide[...] = jnp.zeros_like(wide)
    power = jnp.zeros((side, side), F32)
    for k in range(modes):
        power = power + probe[0, k] * probe[0, k] + probe[1, k] * probe[1, k]
    for s in range(scans):
        row, col = starts[s, 0], starts[s, 1]
        back_row, back_col = lax.rem(full - row, full), lax.rem(full - col, full)
        win = []
        for ch in range(2):
            x = pltpu.roll(obj[ch], back_row, 0)[:side]
            win.append(pltpu.roll(x, back_col, 1)[:, :side])
        wr, wi = win
        ordered = jnp.zeros((side, side), F32)
        for part in split(amp[s]):
            ordered = ordered + dot(order[1], dot(part, order[0]).astype(BF16))
        fars = []
        intensity = jnp.zeros((side, side), F32)
        for k in range(modes):
            pr, pi = probe[0, k], probe[1, k]
            fr, fi = forward(pr * wr - pi * wi, pr * wi + pi * wr, tab)
            intensity = intensity + fr * fr + fi * fi
            fars.append((fr, fi))
        factor = ordered / jnp.maximum(jnp.sqrt(intensity), FLOOR) - 1.0
        gr = jnp.zeros((side, side), F32)
        gi = jnp.zeros((side, side), F32)
        for k in range(modes):
            br, bi = inverse(fars[k][0] * factor, fars[k][1] * factor, tab)
            pr, pi = probe[0, k], probe[1, k]
            gr = gr + pr * br + pi * bi
            gi = gi + pr * bi - pi * br
            for ch, value in enumerate((wr * br + wi * bi, wr * bi - wi * br)):
                at = ch * modes + k
                pgrad[at] = value if s == 0 else pgrad[at] + value
        value = wr * wr + wi * wi
        pgrad[2 * modes] = value if s == 0 else pgrad[2 * modes] + value
        for ch, value in enumerate((gr, gi, power)):
            wide[:side, :side] = value
            x = pltpu.roll(pltpu.roll(wide[...], col, 1), row, 0)
            grad[ch] = x if s == 0 else grad[ch] + x


def step(starts, padded, probe, measured, tab, order):
    side = probe.shape[2]
    full = padded.shape[1]
    vmem = pl.BlockSpec(memory_space=pltpu.VMEM)
    flops = 2 * side**3 * 12 * 8
    return pl.pallas_call(
        step_kernel,
        out_shape=(
            jax.ShapeDtypeStruct((3, full, full), F32),
            jax.ShapeDtypeStruct((2 * probe.shape[1] + 1, side, side), F32),
        ),
        in_specs=[pl.BlockSpec(memory_space=pltpu.SMEM)] + [vmem] * 5,
        out_specs=(vmem, vmem),
        scratch_shapes=[pltpu.VMEM((full, full), F32)],
        compiler_params=pltpu.CompilerParams(vmem_limit_bytes=48 * 1024 * 1024),
        cost_estimate=pl.CostEstimate(flops=flops, bytes_accessed=6 << 20, transcendentals=0),
    )(starts, padded, probe, measured, tab, order)


def local(object_field, probe, amplitudes, offsets):
    tile = object_field.shape[1]
    modes = probe.shape[1]
    side = probe.shape[2]
    half = side // 2
    starts = offsets[0, 0] + half
    measured = amplitudes[0, 0]
    tab = jnp.asarray(tables(side))
    order = jnp.asarray(order_table(side))
    sides = (("row", 1), ("col", 2))
    for _ in range(ITERS):
        padded = padded_2(object_field, sides, half)
        grad, pgrad = step(starts, padded, probe, measured, tab, order)
        total = grad
        for axis, dim in sides:
            count = lax.axis_size(axis)
            low = lax.slice_in_dim(total, 0, half, axis=dim)
            own = lax.slice_in_dim(total, half, half + tile, axis=dim)
            high = lax.slice_in_dim(total, half + tile, 2 * half + tile, axis=dim)
            total = (
                own
                + lax.ppermute(high, axis, [(i, i + 1) for i in range(count - 1)])
                + lax.ppermute(low, axis, [(i + 1, i) for i in range(count - 1)])
            )
        pgrad = lax.psum(pgrad, ("row", "col"))
        summed = pgrad[: 2 * modes].reshape(probe.shape)
        probe = probe + PROBE_STEP * summed / (pgrad[2 * modes] + PROBE_REG)
        object_field = object_field + OBJECT_STEP * total[:2] / (total[2:] + OBJECT_REG)
    return object_field, probe


def solution(mesh):
    return jax.shard_map(
        local,
        mesh=mesh,
        in_specs=(
            P(None, "row", "col"),
            P(),
            P("row", "col", None, None, None),
            P("row", "col", None, None),
        ),
        out_specs=(P(None, "row", "col"), P()),
        check_vma=False,
    )
```

profile of v0, /device:TPU:0, one launch (start us, length us, event | category | flops | bytes accessed | tf_op | source)
XLA Modules:
  0.0 378.3 jit_solution(13250451279664321557)
XLA Ops:
  7.2 4.9 %collective-permute-start = (f32[2,128,128]{2,1,0:T(8,128)}, f32[2,128,128]{2,1,0:T(8,128)S(1)}, u32[]{:S(2)}, u32[]{:S(2)}) collective-permute-start(f32[2,128,128]{2,1,0:T(8,128)} %param.6), channel_id=1, source_target_pairs={{0,4},{4,8},{8,12},{12,16},{16,20},{20,24},{24,28},{1,5},{5,9},{9,... | collective-permute-start | bytes 393224 | tf_op jit(solution)/shard_map/ppermute | solution.py:30
  12.1 1.3 collective-permute-start.1
  13.4 1.7 collective-permute-done
  16.1 3.0 collective-permute-done.1
  19.2 1.4 collective-permute-start.3
  20.6 3.1 collective-permute-start.2
  25.7 11.0 %shard_map.77 = (f32[3,384,384]{2,1,0:T(8,128)}, f32[5,256,256]{2,1,0:T(8,128)}) custom-call(s32[2,2]{1,0:T(2,128)S(1)} %add_bitcast_fusion.starts, f32[2,384,384]{2,1,0:T(8,128)S(1)} %pad_maximum_fusion.obj, f32[2,2,256,256]{3,2,1,0:T(8,128)S(1)} %copy-done, f32[2,256,256]{2,1,0:T(8,128)S(1)} %bitcast.13, bf16[8,256,256]{2,1,0:T(8,128)(2,1)S(1)} %copy-done.2, ...), custom_call_target="tpu_custom_call" | custom-call | flops 3221225472 | bytes 6291456 | tf_op jit(solution)/shard_map/pallas_call | solution.py:169
  36.7 1.3 fusion.11
  38.0 4.3 %collective-permute-start.4 = (f32[3,128,384]{2,1,0:T(8,128)S(1)}, f32[3,128,384]{2,1,0:T(8,128)S(1)}, u32[]{:S(2)}, u32[]{:S(2)}) collective-permute-start(f32[3,128,384]{2,1,0:T(8,128)S(1)} %get-tuple-element.12), channel_id=1, source_target_pairs={{0,4},{4,8},{8,12},{12,16},{16,20},{20,24},{24,28},{1,5},{5,9},{9,... | collective-permute-start | bytes 1769480 | tf_op jit(solution)/shard_map/ppermute | solution.py:204
  42.4 1.3 collective-permute-start.5
  43.7 22.0 %collective-permute-done.4 = f32[3,128,384]{2,1,0:T(8,128)S(1)} collective-permute-done((f32[3,128,384]{2,1,0:T(8,128)S(1)}, f32[3,128,384]{2,1,0:T(8,128)S(1)}, u32[]{:S(2)}, u32[]{:S(2)}) %collective-permute-start.4) | collective-permute-done | bytes 589856 | tf_op jit(solution)/shard_map/ppermute | solution.py:204
  67.0 5.1 %collective-permute-start.6 = (f32[3,128,128]{2,1,0:T(8,128)S(1)}, f32[3,128,128]{2,1,0:T(8,128)S(1)}, u32[]{:S(2)}, u32[]{:S(2)}) collective-permute-start(f32[3,128,128]{2,1,0:T(8,128)S(1)} %get-tuple-element.16), channel_id=1, source_target_pairs={{0,1},{1,2},{2,3},{4,5},{5,6},{6,7},{8,9},{9,10},{10,11},{12,13},{... | collective-permute-start | bytes 589832 | tf_op jit(solution)/shard_map/ppermute | solution.py:204
  72.1 1.3 collective-permute-start.7
  73.5 2.0 collective-permute-done.7
  75.5 1.3 collective-permute-start.9
  76.8 4.8 %collective-permute-start.8 = (f32[2,128,128]{2,1,0:T(8,128)S(1)}, f32[2,128,128]{2,1,0:T(8,128)S(1)}, u32[]{:S(2)}, u32[]{:S(2)}) collective-permute-start(f32[2,128,128]{2,1,0:T(8,128)S(1)} %fusion.7), channel_id=1, source_target_pairs={{0,4},{4,8},{8,12},{12,16},{16,20},{20,24},{24,28},{1,5},{5,9},{9,... | collective-permute-start | bytes 393224 | tf_op jit(solution)/shard_map/ppermute | solution.py:30
  82.7 5.5 %collective-permute-done.8 = f32[2,128,128]{2,1,0:T(8,128)S(1)} collective-permute-done((f32[2,128,128]{2,1,0:T(8,128)S(1)}, f32[2,128,128]{2,1,0:T(8,128)S(1)}, u32[]{:S(2)}, u32[]{:S(2)}) %collective-permute-start.8) | collective-permute-done | bytes 131104 | tf_op jit(solution)/shard_map/ppermute | solution.py:30
  88.9 1.3 collective-permute-start.11
  90.2 4.3 %collective-permute-start.10 = (f32[2,384,128]{2,1,0:T(8,128)}, f32[2,384,128]{2,1,0:T(8,128)}, u32[]{:S(2)}, u32[]{:S(2)}) collective-permute-start(f32[2,384,128]{2,1,0:T(8,128)} %pad_maximum_fusion.2), channel_id=1, source_target_pairs={{0,1},{1,2},{2,3},{4,5},{5,6},{6,7},{8,9},{9,10},{10,11},{12,13},{... | collective-permute-start | bytes 1179656 | tf_op jit(solution)/shard_map/ppermute | solution.py:30
  94.5 113.7 %all-reduce.3.cloned.1.call-done = f32[5,256,256]{2,1,0:T(8,128)} async-done(((f32[5,256,256]{2,1,0:T(8,128)}), f32[5,256,256]{2,1,0:T(8,128)}) %all-reduce.3.cloned.1.call-update) | async-done | bytes 1310736 | tf_op jit(solution)/shard_map/psum | solution.py:207
  209.2 1.2 slice-done.1
  210.6 1.3 pad_maximum_fusion.1.obj
  212.1 11.0 %shard_map.78 = (f32[3,384,384]{2,1,0:T(8,128)}, f32[5,256,256]{2,1,0:T(8,128)}) custom-call(s32[2,2]{1,0:T(2,128)S(1)} %add_bitcast_fusion.starts, f32[2,384,384]{2,1,0:T(8,128)S(1)} %pad_maximum_fusion.1.obj, f32[2,2,256,256]{3,2,1,0:T(8,128)S(1)} %divide_add_fusion.1.probe, f32[2,256,256]{2,1,0:T(8,128)S(1)} %bitcast.14, ...), custom_call_target="tpu_custom_call" | custom-call | flops 3221225472 | bytes 6291456 | tf_op jit(solution)/shard_map/pallas_call | solution.py:169
  223.0 2.1 fusion.10
  225.2 3.4 collective-permute-start.12
  228.5 1.3 collective-permute-start.13
  229.8 25.9 %collective-permute-done.12 = f32[3,128,384]{2,1,0:T(8,128)S(1)} collective-permute-done((f32[3,128,384]{2,1,0:T(8,128)}, f32[3,128,384]{2,1,0:T(8,128)S(1)}, u32[]{:S(2)}, u32[]{:S(2)}) %collective-permute-start.12) | collective-permute-done | bytes 589856 | tf_op jit(solution)/shard_map/ppermute | solution.py:204
  255.7 1.4 add_add_fusion
  257.1 1.3 collective-permute-start.14
  258.5 1.3 collective-permute-start.15
  259.8 107.7 %all-reduce.5.cloned.1.call-done = f32[5,256,256]{2,1,0:T(8,128)} async-done(((f32[5,256,256]{2,1,0:T(8,128)}), f32[5,256,256]{2,1,0:T(8,128)}) %all-reduce.5.cloned.1.call-update) | async-done | bytes 1310736 | tf_op jit(solution)/shard_map/psum | solution.py:207
  368.4 1.2 slice-done
  (47 shorter events, 10.3 us)
Async XLA Ops:
  7.2 201.1 %all-reduce.3.cloned.1.call-start = ((), (), s32[]{:S(2)}) async-start(), calls=%async_computation | async-start | bytes 2621440 | tf_op jit(solution)/shard_map/psum | solution.py:207
  7.2 7.9 %collective-permute-start = (f32[2,128,128]{2,1,0:T(8,128)}, f32[2,128,128]{2,1,0:T(8,128)S(1)}, u32[]{:S(2)}, u32[]{:S(2)}) collective-permute-start(f32[2,128,128]{2,1,0:T(8,128)} %param.6), channel_id=1, source_target_pairs={{0,4},{4,8},{8,12},{12,16},{16,20},{20,24},{24,28},{1,5},{5,9},{9,... | collective-permute-start | bytes 393224 | tf_op jit(solution)/shard_map/ppermute | solution.py:30
  12.1 7.1 %collective-permute-start.1 = (f32[2,128,128]{2,1,0:T(8,128)}, f32[2,128,128]{2,1,0:T(8,128)S(1)}, u32[]{:S(2)}, u32[]{:S(2)}) collective-permute-start(f32[2,128,128]{2,1,0:T(8,128)} %param.6), channel_id=1, source_target_pairs={{4,0},{8,4},{12,8},{16,12},{20,16},{24,20},{28,24},{5,1},{9,5},{13... | collective-permute-start | bytes 393224 | tf_op jit(solution)/shard_map/ppermute | solution.py:32
  15.2 9.9 %copy-start.4 = (bf16[2,256,256]{2,1,0:T(8,128)(2,1)S(1)}, bf16[2,256,256]{2,1,0:T(8,128)(2,1)}, u32[]{:S(2)}) copy-start(bf16[2,256,256]{2,1,0:T(8,128)(2,1)} %constant.12.clone.order) | copy-start | bytes 786436
  19.2 5.9 %copy-start.2 = (bf16[8,256,256]{2,1,0:T(8,128)(2,1)S(1)}, bf16[8,256,256]{2,1,0:T(8,128)(2,1)}, u32[]{:S(2)}) copy-start(bf16[8,256,256]{2,1,0:T(8,128)(2,1)} %constant.4.clone.tab) | copy-start | bytes 3145732
  19.2 5.2 %collective-permute-start.3 = (f32[2,384,128]{2,1,0:T(8,128)S(1)}, f32[2,384,128]{2,1,0:T(8,128)S(1)}, u32[]{:S(2)}, u32[]{:S(2)}) collective-permute-start(f32[2,384,128]{2,1,0:T(8,128)S(1)} %constant_dynamic-update-slice_fusion), channel_id=1, source_target_pairs={{1,0},{2,1},{3,2},{5,4},{6,5},{7,6},{9,8},{10,9},{11,10},{13,12},{... | collective-permute-start | bytes 1179656 | tf_op jit(solution)/shard_map/ppermute | solution.py:32
  20.6 4.4 %collective-permute-start.2 = (f32[2,384,128]{2,1,0:T(8,128)S(1)}, f32[2,384,128]{2,1,0:T(8,128)S(1)}, u32[]{:S(2)}, u32[]{:S(2)}) collective-permute-start(f32[2,384,128]{2,1,0:T(8,128)S(1)} %constant_dynamic-update-slice_fusion), channel_id=1, source_target_pairs={{0,1},{1,2},{2,3},{4,5},{5,6},{6,7},{8,9},{9,10},{10,11},{12,13},{... | collective-permute-start | bytes 1179656 | tf_op jit(solution)/shard_map/ppermute | solution.py:30
  24.4 1.2 copy-start
  24.4 1.4 copy-start.1
  38.0 27.7 %collective-permute-start.4 = (f32[3,128,384]{2,1,0:T(8,128)S(1)}, f32[3,128,384]{2,1,0:T(8,128)S(1)}, u32[]{:S(2)}, u32[]{:S(2)}) collective-permute-start(f32[3,128,384]{2,1,0:T(8,128)S(1)} %get-tuple-element.12), channel_id=1, source_target_pairs={{0,4},{4,8},{8,12},{12,16},{16,20},{20,24},{24,28},{1,5},{5,9},{9,... | collective-permute-start | bytes 1769480 | tf_op jit(solution)/shard_map/ppermute | solution.py:204
  42.4 23.3 %collective-permute-start.5 = (f32[3,128,384]{2,1,0:T(8,128)S(1)}, f32[3,128,384]{2,1,0:T(8,128)S(1)}, u32[]{:S(2)}, u32[]{:S(2)}) collective-permute-start(f32[3,128,384]{2,1,0:T(8,128)S(1)} %get-tuple-element.13), channel_id=1, source_target_pairs={{4,0},{8,4},{12,8},{16,12},{20,16},{24,20},{28,24},{5,1},{9,5},{13... | collective-permute-start | bytes 1769480 | tf_op jit(solution)/shard_map/ppermute | solution.py:205
  67.0 8.5 %copy-start.5 = (f32[2,128,128]{2,1,0:T(8,128)S(1)}, f32[2,128,128]{2,1,0:T(8,128)}, u32[]{:S(2)}) copy-start(f32[2,128,128]{2,1,0:T(8,128)} %param.6) | copy-start | bytes 393220
  67.0 6.5 %collective-permute-start.6 = (f32[3,128,128]{2,1,0:T(8,128)S(1)}, f32[3,128,128]{2,1,0:T(8,128)S(1)}, u32[]{:S(2)}, u32[]{:S(2)}) collective-permute-start(f32[3,128,128]{2,1,0:T(8,128)S(1)} %get-tuple-element.16), channel_id=1, source_target_pairs={{0,1},{1,2},{2,3},{4,5},{5,6},{6,7},{8,9},{9,10},{10,11},{12,13},{... | collective-permute-start | bytes 589832 | tf_op jit(solution)/shard_map/ppermute | solution.py:204
  72.1 3.3 collective-permute-start.7
  73.4 294.0 %all-reduce.5.cloned.1.call-start = ((), (), s32[]{:S(2)}) async-start(), calls=%async_computation.1 | async-start | bytes 2621440 | tf_op jit(solution)/shard_map/psum | solution.py:207
  75.5 7.1 %collective-permute-start.9 = (f32[2,128,128]{2,1,0:T(8,128)S(1)}, f32[2,128,128]{2,1,0:T(8,128)S(1)}, u32[]{:S(2)}, u32[]{:S(2)}) collective-permute-start(f32[2,128,128]{2,1,0:T(8,128)S(1)} %fusion.7), channel_id=1, source_target_pairs={{4,0},{8,4},{12,8},{16,12},{20,16},{24,20},{28,24},{5,1},{9,5},{13... | collective-permute-start | bytes 393224 | tf_op jit(solution)/shard_map/ppermute | solution.py:32
  76.8 11.3 %collective-permute-start.8 = (f32[2,128,128]{2,1,0:T(8,128)S(1)}, f32[2,128,128]{2,1,0:T(8,128)S(1)}, u32[]{:S(2)}, u32[]{:S(2)}) collective-permute-start(f32[2,128,128]{2,1,0:T(8,128)S(1)} %fusion.7), channel_id=1, source_target_pairs={{0,4},{4,8},{8,12},{12,16},{16,20},{20,24},{24,28},{1,5},{5,9},{9,... | collective-permute-start | bytes 393224 | tf_op jit(solution)/shard_map/ppermute | solution.py:30
  88.9 121.7 %collective-permute-start.11 = (f32[2,384,128]{2,1,0:T(8,128)}, f32[2,384,128]{2,1,0:T(8,128)}, u32[]{:S(2)}, u32[]{:S(2)}) collective-permute-start(f32[2,384,128]{2,1,0:T(8,128)} %pad_maximum_fusion.2), channel_id=1, source_target_pairs={{1,0},{2,1},{3,2},{5,4},{6,5},{7,6},{9,8},{10,9},{11,10},{13,12},{... | collective-permute-start | bytes 1179656 | tf_op jit(solution)/shard_map/ppermute | solution.py:32
  90.2 120.4 %collective-permute-start.10 = (f32[2,384,128]{2,1,0:T(8,128)}, f32[2,384,128]{2,1,0:T(8,128)}, u32[]{:S(2)}, u32[]{:S(2)}) collective-permute-start(f32[2,384,128]{2,1,0:T(8,128)} %pad_maximum_fusion.2), channel_id=1, source_target_pairs={{0,1},{1,2},{2,3},{4,5},{5,6},{6,7},{8,9},{9,10},{10,11},{12,13},{... | collective-permute-start | bytes 1179656 | tf_op jit(solution)/shard_map/ppermute | solution.py:30
  209.2 1.2 slice-start.1
  210.6 1.5 copy-start.3
  225.2 30.6 %collective-permute-start.12 = (f32[3,128,384]{2,1,0:T(8,128)}, f32[3,128,384]{2,1,0:T(8,128)S(1)}, u32[]{:S(2)}, u32[]{:S(2)}) collective-permute-start(f32[3,128,384]{2,1,0:T(8,128)} %get-tuple-element.10), channel_id=1, source_target_pairs={{0,4},{4,8},{8,12},{12,16},{16,20},{20,24},{24,28},{1,5},{5,9},{9,... | collective-permute-start | bytes 1769480 | tf_op jit(solution)/shard_map/ppermute | solution.py:204
  228.5 27.2 %collective-permute-start.13 = (f32[3,128,384]{2,1,0:T(8,128)S(1)}, f32[3,128,384]{2,1,0:T(8,128)}, u32[]{:S(2)}, u32[]{:S(2)}) collective-permute-start(f32[3,128,384]{2,1,0:T(8,128)S(1)} %get-tuple-element.11), channel_id=1, source_target_pairs={{4,0},{8,4},{12,8},{16,12},{20,16},{24,20},{28,24},{5,1},{9,5},{13... | collective-permute-start | bytes 1769480 | tf_op jit(solution)/shard_map/ppermute | solution.py:205
  257.1 113.6 %collective-permute-start.14 = (f32[3,128,128]{2,1,0:T(8,128)S(1)}, f32[3,128,128]{2,1,0:T(8,128)S(1)}, u32[]{:S(2)}, u32[]{:S(2)}) collective-permute-start(f32[3,128,128]{2,1,0:T(8,128)S(1)} %get-tuple-element.14), channel_id=1, source_target_pairs={{0,1},{1,2},{2,3},{4,5},{5,6},{6,7},{8,9},{9,10},{10,11},{12,13},{... | collective-permute-start | bytes 589832 | tf_op jit(solution)/shard_map/ppermute | solution.py:204
  258.5 112.3 %collective-permute-start.15 = (f32[3,128,128]{2,1,0:T(8,128)S(1)}, f32[3,128,128]{2,1,0:T(8,128)S(1)}, u32[]{:S(2)}, u32[]{:S(2)}) collective-permute-start(f32[3,128,128]{2,1,0:T(8,128)S(1)} %get-tuple-element.15), channel_id=1, source_target_pairs={{1,0},{2,1},{3,2},{5,4},{6,5},{7,6},{9,8},{10,9},{11,10},{13,12},{... | collective-permute-start | bytes 589832 | tf_op jit(solution)/shard_map/ppermute | solution.py:205
  368.4 1.2 slice-start
Sparse Core Ops, SparseCore 0:
  73.5 134.6 all-reduce.2
  230.0 137.4 all-reduce.4
where the time goes:
time: 379 us; the launch traced here: 378 us
  waiting for transfers between devices  283 us (75%)
  starting transfers between devices  41.7 us (11%)
  Pallas kernels  21.9 us (6%)
  between operations  14.3 us (4%)
  other arithmetic  9.46 us (2%)
  local copies, waits for them, and re-layouts  7.68 us (2%)
    psum x2, waiting for transfers between devices, local(): pgrad = lax.psum(pgrad, ('row', 'col'))  221 us
    ppermute x4, waiting for transfers between devices, local(): lax.ppermute(high, axis, [(i, i + 1) for i in range(count - 1)])  47.9 us
    pallas_call x2, Pallas kernels, step(): pl.pallas_call(step_kernel, out_shape=(jax.ShapeDtypeStruct((3, full, ful...  21.9 us
    ppermute x4, starting transfers between devices, padded_2(): lax.ppermute(tail, axis, [(i, (i + 1) % count) for i in range(ends)])  17.1 us
    ppermute x4, starting transfers between devices, local(): lax.ppermute(high, axis, [(i, i + 1) for i in range(count - 1)])  14.1 us
    ppermute x4, waiting for transfers between devices, padded_2(): lax.ppermute(tail, axis, [(i, (i + 1) % count) for i in range(ends)])  7.84 us
  transfers between devices with their start and end apart: 18, of which 10 were waited for; matrix products, arithmetic and copies ran while one was open for 2% of the time, Pallas kernels for 0%

commit v1 on v0

--- a/solution.py
+++ b/solution.py
@@ -19,21 +19,303 @@
 BF16 = jnp.bfloat16
 
 
-def padded_2(cells, sides, width):
-    for axis, dim in sides:
-        count = lax.axis_size(axis)
-        ends = count - 1
-        head = lax.slice_in_dim(cells, 0, width, axis=dim)
-        tail = lax.slice_in_dim(cells, cells.shape[dim] - width, cells.shape[dim], axis=dim)
-        cells = jnp.concatenate(
-            [
-                lax.ppermute(tail, axis, [(i, (i + 1) % count) for i in range(ends)]),
-                cells,
-                lax.ppermute(head, axis, [((i + 1) % count, i) for i in range(ends)]),
-            ],
-            axis=dim,
+MESH = pl.DeviceIdType.MESH
+
+
+def bits_of(axis, count):
+    return [(axis, b) for b in range(count.bit_length() - 1)]
+
+
+def stream_orders(rows, cols):
+    row_bits, col_bits = bits_of("row", rows), bits_of("col", cols)
+    one = col_bits + row_bits
+    two = col_bits[:1] + row_bits[1:-1] + col_bits[1:] + row_bits[:1] + row_bits[-1:]
+    return (one, two)
+
+
+def plan(order, count):
+    steps = []
+    for axis, bit in order:
+        halves = count % 2 == 0
+        steps.append((axis, bit, count, halves))
+        count = count // 2 if halves else count
+    return steps
+
+
+def bit_and_partner(axis, bit):
+    me = lax.axis_index(axis)
+    mine = lax.rem(me // (1 << bit), 2)
+    return mine, {axis: me + (1 << bit) * (1 - 2 * mine)}
+
+
+def remote(src, dst, sems, at, device):
+    return pltpu.make_async_remote_copy(
+        src_ref=src, dst_ref=dst, send_sem=sems.at[0, at], recv_sem=sems.at[1, at],
+        device_id=device, device_id_type=MESH,
+    )
+
+
+def greet(rows, cols, bits):
+    barrier = pltpu.get_barrier_semaphore()
+    row, col = lax.axis_index("row"), lax.axis_index("col")
+    devices = [
+        {"row": lax.rem(row + 1, rows)}, {"row": lax.rem(row + rows - 1, rows)},
+        {"col": lax.rem(col + 1, cols)}, {"col": lax.rem(col + cols - 1, cols)},
+    ] + [bit_and_partner(axis, bit)[1] for axis, bit in bits]
+    for device in devices:
+        pl.semaphore_signal(barrier, inc=1, device_id=device, device_id_type=MESH)
+    pl.semaphore_wait(barrier, len(devices))
+
+
+class Pair:
+    def __init__(self, axis, count, sems, at, up, down):
+        me = lax.axis_index(axis)
+        self.not_last, self.not_first = me < count - 1, me > 0
+        self.up = remote(up[0], up[1], sems, at, {axis: jnp.minimum(me + 1, count - 1)})
+        self.down = remote(down[0], down[1], sems, at + 1, {axis: jnp.maximum(me - 1, 0)})
+
+    def start(self):
+        pl.when(self.not_last)(self.up.start)
+        pl.when(self.not_first)(self.down.start)
+
+    def wait(self):
+        pl.when(self.not_first)(self.up.wait_recv)
+        pl.when(self.not_last)(self.down.wait_recv)
+
+    def wait_sent(self):
+        pl.when(self.not_last)(self.up.wait_send)
+        pl.when(self.not_first)(self.down.wait_send)
+
+
+def row_halo(tile_ref, pad, sems, at, rows, tile, half):
+    own = pl.ds(half, tile)
+    return Pair(
+        "row", rows, sems, at,
+        (tile_ref, pad.at[:, pl.ds(0, half), own]),
+        (tile_ref, pad.at[:, pl.ds(half + tile, half), own]),
+    )
+
+
+def col_halo(pad, sems, at, cols, tile, half):
+    own = pl.ds(half, tile)
+    return Pair(
+        "col", cols, sems, at,
+        (pad.at[:, :, own], pad.at[:, :, pl.ds(0, half)]),
+        (pad.at[:, :, own], pad.at[:, :, pl.ds(half + tile, half)]),
+    )
+
+
+def clear_rim(pad, rows, cols, tile, half):
+    row, col = lax.axis_index("row"), lax.axis_index("col")
+    own = pl.ds(half, tile)
+
+    def clear(*where):
+        def run():
+            pad[where] = jnp.zeros_like(pad[where])
+        return run
+
+    every = slice(None)
+    pl.when(row == 0)(clear(every, pl.ds(0, half), own))
+    pl.when(row == rows - 1)(clear(every, pl.ds(half + tile, half), own))
+    pl.when(col == 0)(clear(every, every, pl.ds(0, half)))
+    pl.when(col == cols - 1)(clear(every, every, pl.ds(half + tile, half)))
+
+
+def halo_kernel(rows, cols, obj, out, pad, sems):
+    tile = obj.shape[1]
+    half = (pad.shape[1] - tile) // 2
+    greet(rows, cols, ())
+    by_row = row_halo(obj, pad, sems, 0, rows, tile, half)
+    by_row.start()
+    clear_rim(pad, rows, cols, tile, half)
+    pad[:, pl.ds(half, tile), pl.ds(half, tile)] = obj[...]
+    by_row.wait()
+    by_col = col_halo(pad, sems, 2, cols, tile, half)
+    by_col.start()
+    by_col.wait()
+    by_row.wait_sent()
+    by_col.wait_sent()
+    out[...] = pad[...]
+
+
+def halo(rows, cols, obj, half):
+    full = obj.shape[1] + 2 * half
+    vmem = pl.BlockSpec(memory_space=pltpu.VMEM)
+    return pl.pallas_call(
+        lambda *refs: halo_kernel(rows, cols, *refs),
+        out_shape=jax.ShapeDtypeStruct((2, full, full), F32),
+        in_specs=[vmem],
+        out_specs=vmem,
+        scratch_shapes=[pltpu.VMEM((2, full, full), F32), pltpu.SemaphoreType.DMA((2, 4))],
+        compiler_params=pltpu.CompilerParams(
+            collective_id=0, has_side_effects=True, vmem_limit_bytes=32 * 1024 * 1024
+        ),
+    )(obj)
+
+
+def exchange_kernel(rows, cols, last, obj, probe, grad, pgrad, *refs):
+    if last:
+        obj_out, probe_out, colbuf, mid, rowbuf, new_obj, acc, inbox, res, gsems, rsems, asems = refs
+    else:
+        (obj_out, probe_out, pad_out, colbuf, mid, rowbuf, new_obj, acc, inbox, res,
+         gsems, rsems, asems, pad, hsems) = refs
+    tile = obj.shape[1]
+    full = grad.shape[1]
+    half = (full - tile) // 2
+    row, col = lax.axis_index("row"), lax.axis_index("col")
+    orders = stream_orders(rows, cols)
+    greet(rows, cols, orders[0])
+    spots = pgrad.shape[0] // len(orders)
+    plans = [plan(order, spots) for order in orders]
+    los = [s * spots for s in range(len(orders))]
+    box = 0
+    reduces, gathers = [], []
+    for s, steps in enumerate(plans):
+        for step, (axis, bit, count, halves) in enumerate(steps):
+            n = count // 2 if halves else count
+            mine, device = bit_and_partner(axis, bit)
+            lo = los[s]
+            keep = lo + mine * n if halves else lo
+            send = lo + (1 - mine) * n if halves else lo
+            source = pgrad if step == 0 else acc
+            buf = inbox.at[pl.ds(box, n)]
+            box += n
+            copy = remote(source.at[pl.ds(send, n)], buf, rsems.at[s], step, device)
+            reduces.append((step, copy, source, keep, n, buf))
+            if halves:
+                span = res.at[pl.ds(keep, n)]
+                gathers.append((s, step, remote(span, span, asems.at[s], step, device)))
+                los[s] = keep
+
+    def start_reduce(at):
+        for step, copy, *_ in reduces:
+            if step == at:
+                copy.start()
+
+    def finish_reduce(at):
+        for step, copy, source, keep, n, buf in reduces:
+            if step == at:
+                copy.wait()
+                acc[pl.ds(keep, n)] = source[pl.ds(keep, n)] + buf[...]
+
+    total_steps = len(plans[0])
+    start_reduce(0)
+    by_col = Pair(
+        "col", cols, gsems, 0,
+        (grad.at[:, :, pl.ds(half + tile, half)], colbuf.at[0]),
+        (grad.at[:, :, pl.ds(0, half)], colbuf.at[1]),
+    )
+    by_row = Pair(
+        "row", rows, gsems, 2,
+        (mid.at[:, pl.ds(half + tile, half)], rowbuf.at[0]),
+        (mid.at[:, pl.ds(0, half)], rowbuf.at[1]),
+    )
+    by_col.start()
+
+    def clear(ref, at):
+        def run():
+            ref[at] = jnp.zeros_like(ref[at])
+        return run
+
+    pl.when(col == 0)(clear(colbuf, 0))
+    pl.when(col == cols - 1)(clear(colbuf, 1))
+    pl.when(row == 0)(clear(rowbuf, 0))
+    pl.when(row == rows - 1)(clear(rowbuf, 1))
+    if not last:
+        clear_rim(pad, rows, cols, tile, half)
+
+    finish_reduce(0)
+    start_reduce(1)
+    by_col.wait()
+    mid[...] = grad[:, :, half:half + tile] + colbuf[0] + colbuf[1]
+    by_row.start()
+    finish_reduce(1)
+    start_reduce(2)
+    by_row.wait()
+    total = mid[:, half:half + tile] + rowbuf[0] + rowbuf[1]
+    new = obj[...] + OBJECT_STEP * total[:2] / (total[2:] + OBJECT_REG)
+    new_obj[...] = new
+    obj_out[...] = new
+    if not last:
+        halo_row = row_halo(new_obj, pad, hsems, 0, rows, tile, half)
+        halo_col = col_halo(pad, hsems, 2, cols, tile, half)
+        halo_row.start()
+        pad[:, pl.ds(half, tile), pl.ds(half, tile)] = new
+    finish_reduce(2)
+    start_reduce(3)
+    if not last:
+        halo_row.wait()
+        halo_col.start()
+    for step in range(3, total_steps):
+        finish_reduce(step)
+        if step + 1 < total_steps:
+            start_reduce(step + 1)
+    for s, steps in enumerate(plans):
+        _, _, count, halves = steps[-1]
+        n = count // 2 if halves else count
+        span = pl.ds(los[s], n)
+        terms = acc[span]
+        channels = probe.shape[1]
+        res[span] = probe[span] + PROBE_STEP * terms[:, :channels] / (
+            terms[:, channels:] + PROBE_REG
         )
-    return cells
+    for at in reversed(range(total_steps)):
+        now = [copy for s, step, copy in gathers if step == at]
+        for copy in now:
+            copy.start()
+        for copy in now:
+            copy.wait()
+    by_col.wait_sent()
+    by_row.wait_sent()
+    probe_out[...] = res[...]
+    if not last:
+        halo_col.wait()
+        halo_row.wait_sent()
+        halo_col.wait_sent()
+        pad_out[...] = pad[...]
+
+
+def exchange(rows, cols, last, obj, probe, grad, pgrad):
+    tile, full = obj.shape[1], grad.shape[1]
+    half = (full - tile) // 2
+    channels = grad.shape[0]
+    orders = stream_orders(rows, cols)
+    spots = pgrad.shape[0] // len(orders)
+    boxes = sum(
+        count // 2 if halves else count
+        for order in orders
+        for _, _, count, halves in plan(order, spots)
+    )
+    steps = len(orders[0])
+    vmem = pl.BlockSpec(memory_space=pltpu.VMEM)
+    out_shape = [jax.ShapeDtypeStruct(obj.shape, F32), jax.ShapeDtypeStruct(probe.shape, F32)]
+    scratch = [
+        pltpu.VMEM((2, channels, full, half), F32),
+        pltpu.VMEM((channels, full, tile), F32),
+        pltpu.VMEM((2, channels, half, tile), F32),
+        pltpu.VMEM(obj.shape, F32),
+        pltpu.VMEM(pgrad.shape, F32),
+        pltpu.VMEM((boxes,) + pgrad.shape[1:], F32),
+        pltpu.VMEM(probe.shape, F32),
+        pltpu.SemaphoreType.DMA((2, 4)),
+        pltpu.SemaphoreType.DMA((len(orders), 2, steps)),
+        pltpu.SemaphoreType.DMA((len(orders), 2, steps)),
+    ]
+    if not last:
+        out_shape.append(jax.ShapeDtypeStruct((2, full, full), F32))
+        scratch += [pltpu.VMEM((2, full, full), F32), pltpu.SemaphoreType.DMA((2, 4))]
+    return pl.pallas_call(
+        lambda *refs: exchange_kernel(rows, cols, last, *refs),
+        out_shape=out_shape,
+        in_specs=[vmem] * 4,
+        out_specs=[vmem] * len(out_shape),
+        scratch_shapes=scratch,
+        compiler_params=pltpu.CompilerParams(
+            collective_id=2 if last else 1,
+            has_side_effects=True,
+            vmem_limit_bytes=48 * 1024 * 1024,
+        ),
+    )(obj, probe, grad, pgrad)
 
 
 def split_np(table):
@@ -115,11 +397,29 @@
     )
 
 
-def step_kernel(starts, obj, probe, amp, tab, order, grad, pgrad, wide):
-    side = probe.shape[2]
+def whole(tiles, at, side):
+    blocks = tiles.shape[0] * tiles.shape[2] // side
+    per = tiles.shape[0] // blocks
+    return jnp.concatenate(
+        [tiles[j * per:(j + 1) * per, at].reshape(side, -1) for j in range(blocks)], 1
+    )
+
+
+def put(tiles, at, value, add):
+    width = tiles.shape[3]
+    per = value.shape[0] // tiles.shape[2]
+    for j in range(value.shape[1] // width):
+        part = value[:, j * width:(j + 1) * width].reshape(per, tiles.shape[2], width)
+        span = slice(j * per, (j + 1) * per)
+        tiles[span, at] = tiles[span, at] + part if add else part
+
+
+def step_kernel(starts, obj, tiles, amp, tab, order, grad, pgrad, wide):
+    side = amp.shape[1]
     full = obj.shape[1]
-    modes = probe.shape[1]
+    modes = tiles.shape[1] // 2
     scans = amp.shape[0]
+    probe = {(c, k): whole(tiles, c * modes + k, side) for c in range(2) for k in range(modes)}
     wide[...] = jnp.zeros_like(wide)
     power = jnp.zeros((side, side), F32)
     for k in range(modes):
@@ -152,9 +452,8 @@
             gi = gi + pr * bi - pi * br
             for ch, value in enumerate((wr * br + wi * bi, wr * bi - wi * br)):
                 at = ch * modes + k
-                pgrad[at] = value if s == 0 else pgrad[at] + value
-        value = wr * wr + wi * wi
-        pgrad[2 * modes] = value if s == 0 else pgrad[2 * modes] + value
+                put(pgrad, at, value, s > 0)
+        put(pgrad, 2 * modes, wr * wr + wi * wi, s > 0)
         for ch, value in enumerate((gr, gi, power)):
             wide[:side, :side] = value
             x = pltpu.roll(pltpu.roll(wide[...], col, 1), row, 0)
@@ -162,7 +461,7 @@
 
 
 def step(starts, padded, probe, measured, tab, order):
-    side = probe.shape[2]
+    side = measured.shape[1]
     full = padded.shape[1]
     vmem = pl.BlockSpec(memory_space=pltpu.VMEM)
     flops = 2 * side**3 * 12 * 8
@@ -170,7 +469,7 @@
         step_kernel,
         out_shape=(
             jax.ShapeDtypeStruct((3, full, full), F32),
-            jax.ShapeDtypeStruct((2 * probe.shape[1] + 1, side, side), F32),
+            jax.ShapeDtypeStruct((probe.shape[0], probe.shape[1] + 1) + probe.shape[2:], F32),
         ),
         in_specs=[pl.BlockSpec(memory_space=pltpu.SMEM)] + [vmem] * 5,
         out_specs=(vmem, vmem),
@@ -181,34 +480,26 @@
 
 
 def local(object_field, probe, amplitudes, offsets):
-    tile = object_field.shape[1]
-    modes = probe.shape[1]
     side = probe.shape[2]
     half = side // 2
+    rows, cols = lax.axis_size("row"), lax.axis_size("col")
     starts = offsets[0, 0] + half
     measured = amplitudes[0, 0]
     tab = jnp.asarray(tables(side))
     order = jnp.asarray(order_table(side))
-    sides = (("row", 1), ("col", 2))
-    for _ in range(ITERS):
-        padded = padded_2(object_field, sides, half)
-        grad, pgrad = step(starts, padded, probe, measured, tab, order)
-        total = grad
-        for axis, dim in sides:
-            count = lax.axis_size(axis)
-            low = lax.slice_in_dim(total, 0, half, axis=dim)
-            own = lax.slice_in_dim(total, half, half + tile, axis=dim)
-            high = lax.slice_in_dim(total, half + tile, 2 * half + tile, axis=dim)
-            total = (
-                own
-                + lax.ppermute(high, axis, [(i, i + 1) for i in range(count - 1)])
-                + lax.ppermute(low, axis, [(i + 1, i) for i in range(count - 1)])
-            )
-        pgrad = lax.psum(pgrad, ("row", "col"))
-        summed = pgrad[: 2 * modes].reshape(probe.shape)
-        probe = probe + PROBE_STEP * summed / (pgrad[2 * modes] + PROBE_REG)
-        object_field = object_field + OBJECT_STEP * total[:2] / (total[2:] + OBJECT_REG)
-    return object_field, probe
+    channels = probe.shape[0] * probe.shape[1]
+    cut = (channels, side // 8, 8, side // 128, 128)
+    tiles = probe.reshape(cut).transpose(3, 1, 0, 2, 4).reshape(-1, channels, 8, 128)
+    padded = halo(rows, cols, object_field, half)
+    for iteration in range(ITERS):
+        last = iteration + 1 == ITERS
+        grad, pgrad = step(starts, padded, tiles, measured, tab, order)
+        out = exchange(rows, cols, last, object_field, tiles, grad, pgrad)
+        object_field, tiles = out[:2]
+        if not last:
+            padded = out[2]
+    back = tiles.reshape(side // 128, side // 8, channels, 8, 128).transpose(2, 1, 3, 0, 4)
+    return object_field, back.reshape(probe.shape)
 
 
 def solution(mesh):

time: 379 us -> 139 us (0.37)
  waiting for transfers between devices: 283 us -> 0 us
  Pallas kernels: 21.9 us -> 133 us
  starting transfers between devices: 41.7 us -> 0 us
  between operations: 14.3 us -> 0.71 us
  other arithmetic: 9.46 us -> 0.72 us
    psum x2 -> x0, waiting for transfers between devices: 221 us -> none  [local(): pgrad = lax.psum(pgrad, ('row', 'col'))]
    pallas_call x0 -> x3, Pallas kernels: none -> 110 us  [the longest x2 100 us: exchange(): pl.pallas_call(lambda *refs: exchange_kernel(rows, cols, last, *refs), ou...]
    ppermute x16 -> x0, waiting for transfers between devices: 61.8 us -> none  [the longest x4 47.9 us: local(): lax.ppermute(high, axis, [(i, i + 1) for i in range(count - 1)])]
    ppermute x16 -> x0, starting transfers between devices: 41.7 us -> none  [the longest x4 17.1 us: padded_2(): lax.ppermute(tail, axis, [(i, (i + 1) % count) for i in range(ends)])]
    add x10 -> x0, other arithmetic: 6.59 us -> none  [the longest x4 3.21 us: local(): probe = probe + PROBE_STEP * summed / (pgrad[2 * modes] + PROBE_REG)]
    slice x8 -> x0, local copies, waits for them, and re-layouts: 5.94 us -> none  [the longest x4 3.51 us: local(): high = lax.slice_in_dim(total, half + tile, 2 * half + tile, axis=dim)]
  transfers between devices with their start and end apart: 18 -> 0, of which waited for: 10 -> 0; matrix products, arithmetic and copies ran while one was open for 2% -> 0% of each run, Pallas kernels for 0% -> 0%
where the time goes in v1:
time: 139 us
  Pallas kernels  133 us (96%)
  local copies, waits for them, and re-layouts  4.69 us (3%)
    pallas_call x2, Pallas kernels, exchange(): pl.pallas_call(lambda *refs: exchange_kernel(rows, cols, last, *refs), ou...  100 us
    pallas_call x2, Pallas kernels, step(): pl.pallas_call(step_kernel, out_shape=(jax.ShapeDtypeStruct((3, full, ful...  22.3 us
    pallas_call x1, Pallas kernels, halo(): pl.pallas_call(lambda *refs: halo_kernel(rows, cols, *refs), out_shape=ja...  10.3 us

profile of v1, /device:TPU:0, one launch (start us, length us, event | category | flops | bytes accessed | tf_op | source)
XLA Modules:
  0.0 138.6 jit_solution(5446122665766857787)
XLA Ops:
  0.6 0.0 copy-start.1
  0.6 0.7 add_bitcast_fusion.starts
  1.4 0.0 copy-start.2
  1.4 0.0 copy-start.3
  1.4 0.0 copy-start.4
  1.4 1.5 %copy.8 = f32[4,32,8,2,128]{4,2,0,1,3:T(8,128)S(1)} copy(f32[4,32,8,2,128]{4,2,3,1,0:T(8,128)} %bitcast.16) | data formatting | bytes 2097152 | tf_op jit(solution)/shard_map/reshape | solution.py:492
  2.9 0.0 copy-done.1
  2.9 10.3 %shard_map.77.obj = f32[2,384,384]{2,1,0:T(8,128)S(1)} custom-call(f32[2,128,128]{2,1,0:T(8,128)S(1)} %copy-done.1), custom_call_target="tpu_custom_call" | custom-call | tf_op jit(solution)/shard_map/pallas_call | solution.py:144
  13.1 0.0 copy-done.2
  13.1 0.0 copy-done.3
  13.1 0.0 copy-done.4
  13.2 11.2 %shard_map.78 = (f32[3,384,384]{2,1,0:T(8,128)}, f32[64,5,8,128]{3,2,1,0:T(8,128)S(1)}) custom-call(s32[2,2]{1,0:T(2,128)S(1)} %add_bitcast_fusion.starts, f32[2,384,384]{2,1,0:T(8,128)S(1)} %shard_map.77.obj, f32[64,4,8,128]{3,2,1,0:T(8,128)S(1)} %bitcast.11, f32[2,256,256]{2,1,0:T(8,128)S(1)} %bitcast.14, bf16[8,256,256]{2,1,0:T(8,128)(2,1)S(1)} %copy-done.3, ...), custom_call_target="tpu_custom_call" | custom-call | flops 3221225472 | bytes 6291456 | tf_op jit(solution)/shard_map/pallas_call | solution.py:468
  24.3 57.0 %shard_map.79 = (f32[2,128,128]{2,1,0:T(8,128)S(1)}, f32[64,4,8,128]{3,2,1,0:T(8,128)S(1)}, f32[2,384,384]{2,1,0:T(8,128)S(1)}) custom-call(f32[2,128,128]{2,1,0:T(8,128)S(1)} %copy-done.1, f32[64,4,8,128]{3,2,1,0:T(8,128)S(1)} %bitcast.12, f32[3,384,384]{2,1,0:T(8,128)} %get-tuple-element.11.refs_2_, f32[64,5,8,128]{3,2,1,0:T(8,128)S(1)} %get-tuple-element.12.refs_3_), custom_call_target="tpu_custom_call" | custom-call | tf_op jit(solution)/shard_map/pallas_call | solution.py:307
  81.3 11.1 %shard_map.80 = (f32[3,384,384]{2,1,0:T(8,128)}, f32[64,5,8,128]{3,2,1,0:T(8,128)S(1)}) custom-call(s32[2,2]{1,0:T(2,128)S(1)} %add_bitcast_fusion.starts, f32[2,384,384]{2,1,0:T(8,128)S(1)} %get-tuple-element.15.obj, f32[64,4,8,128]{3,2,1,0:T(8,128)S(1)} %get-tuple-element.14.tiles.refs_1_, f32[2,256,256]{2,1,0:T(8,128)S(1)} %bitcast.15, ...), custom_call_target="tpu_custom_call" | custom-call | flops 3221225472 | bytes 6291456 | tf_op jit(solution)/shard_map/pallas_call | solution.py:468
  92.5 0.0 copy-start
  92.5 1.5 %copy-done = f32[3,384,384]{2,1,0:T(8,128)S(1)} copy-done((f32[3,384,384]{2,1,0:T(8,128)S(1)}, f32[3,384,384]{2,1,0:T(8,128)}, u32[]{:S(2)}) %copy-start) | copy-done | bytes 1769496
  93.9 43.0 %shard_map.81 = (f32[2,128,128]{2,1,0:T(8,128)S(1)}, f32[64,4,8,128]{3,2,1,0:T(8,128)S(1)}) custom-call(f32[2,128,128]{2,1,0:T(8,128)S(1)} %get-tuple-element.13.refs_0_, f32[64,4,8,128]{3,2,1,0:T(8,128)S(1)} %get-tuple-element.14.tiles.refs_1_, f32[3,384,384]{2,1,0:T(8,128)S(1)} %copy-done, f32[64,5,8,128]{3,2,1,0:T(8,128)S(1)} %get-tuple-element.17.refs_3_), custom_call_target="tpu_custom_call" | custom-call | tf_op jit(solution)/shard_map/pallas_call | solution.py:307
  136.9 1.1 copy.9
  138.0 0.7 copy.11
Async XLA Ops:
  0.6 2.2 %copy-start.1 = (f32[2,128,128]{2,1,0:T(8,128)S(1)}, f32[2,128,128]{2,1,0:T(8,128)}, u32[]{:S(2)}) copy-start(f32[2,128,128]{2,1,0:T(8,128)} %refs_0_.3) | copy-start | bytes 393220
  1.4 11.8 %copy-start.2 = (f32[1,1,2,256,256]{4,3,2,1,0:T(8,128)S(1)}, f32[1,1,2,256,256]{4,3,2,1,0:T(8,128)}, u32[]{:S(2)}) copy-start(f32[1,1,2,256,256]{4,3,2,1,0:T(8,128)} %param.8) | copy-start | bytes 1572868
  1.4 11.8 %copy-start.3 = (bf16[8,256,256]{2,1,0:T(8,128)(2,1)S(1)}, bf16[8,256,256]{2,1,0:T(8,128)(2,1)}, u32[]{:S(2)}) copy-start(bf16[8,256,256]{2,1,0:T(8,128)(2,1)} %constant.6.clone.tab) | copy-start | bytes 3145732
  1.4 11.8 %copy-start.4 = (bf16[2,256,256]{2,1,0:T(8,128)(2,1)S(1)}, bf16[2,256,256]{2,1,0:T(8,128)(2,1)}, u32[]{:S(2)}) copy-start(bf16[2,256,256]{2,1,0:T(8,128)(2,1)} %constant.7.clone.order) | copy-start | bytes 786436
  92.5 1.5 %copy-start = (f32[3,384,384]{2,1,0:T(8,128)S(1)}, f32[3,384,384]{2,1,0:T(8,128)}, u32[]{:S(2)}) copy-start(f32[3,384,384]{2,1,0:T(8,128)} %get-tuple-element.16.refs_2_) | copy-start | bytes 5308420

commit v2 on v1

--- a/solution.py
+++ b/solution.py
@@ -17,6 +17,8 @@
 PROBE_REG = 1.0
 F32 = jnp.float32
 BF16 = jnp.bfloat16
+STREAMS = 2
+ABSENT = 1 << 20
 
 
 MESH = pl.DeviceIdType.MESH
@@ -26,42 +28,54 @@
     return [(axis, b) for b in range(count.bit_length() - 1)]
 
 
-def stream_orders(rows, cols):
+def phases(rows, cols):
     row_bits, col_bits = bits_of("row", rows), bits_of("col", cols)
-    one = col_bits + row_bits
-    two = col_bits[:1] + row_bits[1:-1] + col_bits[1:] + row_bits[:1] + row_bits[-1:]
-    return (one, two)
-
-
-def plan(order, count):
+    rest = row_bits[1:] + col_bits[2:]
+    groups = [col_bits[:1], col_bits[1:2] + row_bits[:1]]
+    return groups + [rest[i:i + 2] for i in range(0, len(rest), 2)]
+
+
+def plan(groups, count):
     steps = []
-    for axis, bit in order:
-        halves = count % 2 == 0
-        steps.append((axis, bit, count, halves))
-        count = count // 2 if halves else count
+    for group in groups:
+        if count % (1 << len(group)) == 0:
+            count //= 1 << len(group)
+            steps.append((group, True, count))
+        else:
+            steps += [([bit], False, count) for bit in group]
     return steps
 
 
-def bit_and_partner(axis, bit):
-    me = lax.axis_index(axis)
-    mine = lax.rem(me // (1 << bit), 2)
-    return mine, {axis: me + (1 << bit) * (1 - 2 * mine)}
+def peer(group, mask):
+    device, mine, theirs = {}, 0, 0
+    for i, (axis, bit) in enumerate(group):
+        me = lax.axis_index(axis)
+        held = lax.rem(me // (1 << bit), 2)
+        mine = mine + held * (1 << i)
+        if mask >> i & 1:
+            device[axis] = device.get(axis, me) + (1 << bit) * (1 - 2 * held)
+            theirs = theirs + (1 - held) * (1 << i)
+        else:
+            theirs = theirs + held * (1 << i)
+    return device, mine, theirs
 
 
 def remote(src, dst, sems, at, device):
     return pltpu.make_async_remote_copy(
-        src_ref=src, dst_ref=dst, send_sem=sems.at[0, at], recv_sem=sems.at[1, at],
+        src_ref=src, dst_ref=dst, send_sem=sems.at[(0,) + at], recv_sem=sems.at[(1,) + at],
         device_id=device, device_id_type=MESH,
     )
 
 
-def greet(rows, cols, bits):
+def greet(rows, cols, groups):
     barrier = pltpu.get_barrier_semaphore()
     row, col = lax.axis_index("row"), lax.axis_index("col")
     devices = [
         {"row": lax.rem(row + 1, rows)}, {"row": lax.rem(row + rows - 1, rows)},
         {"col": lax.rem(col + 1, cols)}, {"col": lax.rem(col + cols - 1, cols)},
-    ] + [bit_and_partner(axis, bit)[1] for axis, bit in bits]
+    ]
+    for group in groups:
+        devices += [peer(group, mask)[0] for mask in range(1, 1 << len(group))]
     for device in devices:
         pl.semaphore_signal(barrier, inc=1, device_id=device, device_id_type=MESH)
     pl.semaphore_wait(barrier, len(devices))
@@ -71,8 +85,8 @@
     def __init__(self, axis, count, sems, at, up, down):
         me = lax.axis_index(axis)
         self.not_last, self.not_first = me < count - 1, me > 0
-        self.up = remote(up[0], up[1], sems, at, {axis: jnp.minimum(me + 1, count - 1)})
-        self.down = remote(down[0], down[1], sems, at + 1, {axis: jnp.maximum(me - 1, 0)})
+        self.up = remote(up[0], up[1], sems, (at,), {axis: jnp.minimum(me + 1, count - 1)})
+        self.down = remote(down[0], down[1], sems, (at + 1,), {axis: jnp.maximum(me - 1, 0)})
 
     def start(self):
         pl.when(self.not_last)(self.up.start)
@@ -121,39 +135,94 @@
     pl.when(col == cols - 1)(clear(every, every, pl.ds(half + tile, half)))
 
 
-def halo_kernel(rows, cols, obj, out, pad, sems):
+def halo_kernel(rows, cols, obj, offs, out, near_out, pad, near, sems):
     tile = obj.shape[1]
     half = (pad.shape[1] - tile) // 2
     greet(rows, cols, ())
     by_row = row_halo(obj, pad, sems, 0, rows, tile, half)
     by_row.start()
+    offs_row = Pair("row", rows, sems, 4, (offs, near.at[1, 0]), (offs, near.at[1, 2]))
+    offs_row.start()
+    near[1, 1] = offs[...]
+    row, col = lax.axis_index("row"), lax.axis_index("col")
+
+    def absent(*where):
+        def run():
+            near[where] = jnp.full_like(near[where], ABSENT)
+        return run
+
+    pl.when(row == 0)(absent(1, 0))
+    pl.when(row == rows - 1)(absent(1, 2))
+    pl.when(col == 0)(absent(0))
+    pl.when(col == cols - 1)(absent(2))
     clear_rim(pad, rows, cols, tile, half)
     pad[:, pl.ds(half, tile), pl.ds(half, tile)] = obj[...]
     by_row.wait()
     by_col = col_halo(pad, sems, 2, cols, tile, half)
     by_col.start()
+    offs_row.wait()
+    offs_col = Pair("col", cols, sems, 6, (near.at[1], near.at[0]), (near.at[1], near.at[2]))
+    offs_col.start()
     by_col.wait()
-    by_row.wait_sent()
-    by_col.wait_sent()
+    offs_col.wait()
+    for pair in (by_row, by_col, offs_row, offs_col):
+        pair.wait_sent()
     out[...] = pad[...]
-
-
-def halo(rows, cols, obj, half):
+    near_out[...] = near[...]
+
+
+def halo(rows, cols, obj, offs, half):
     full = obj.shape[1] + 2 * half
     vmem = pl.BlockSpec(memory_space=pltpu.VMEM)
     return pl.pallas_call(
         lambda *refs: halo_kernel(rows, cols, *refs),
-        out_shape=jax.ShapeDtypeStruct((2, full, full), F32),
-        in_specs=[vmem],
-        out_specs=vmem,
-        scratch_shapes=[pltpu.VMEM((2, full, full), F32), pltpu.SemaphoreType.DMA((2, 4))],
+        out_shape=(
+            jax.ShapeDtypeStruct((2, full, full), F32),
+            jax.ShapeDtypeStruct((3, 3) + offs.shape, jnp.int32),
+        ),
+        in_specs=[vmem, vmem],
+        out_specs=(vmem, vmem),
+        scratch_shapes=[
+            pltpu.VMEM((2, full, full), F32),
+            pltpu.VMEM((3, 3) + offs.shape, jnp.int32),
+            pltpu.SemaphoreType.DMA((2, 8)),
+        ],
         compiler_params=pltpu.CompilerParams(
             collective_id=0, has_side_effects=True, vmem_limit_bytes=32 * 1024 * 1024
         ),
-    )(obj)
-
-
-def exchange_kernel(rows, cols, last, obj, probe, grad, pgrad, *refs):
+    )(obj, offs)
+
+
+def weight_of(probe, near, scans, tile):
+    channels = probe.shape[1]
+    power = probe[:, 0] * probe[:, 0]
+    for at in range(1, channels):
+        power = power + probe[:, at] * probe[:, at]
+    side = math.isqrt(power.size)
+    power = whole(power[:, None], 0, side)
+    both = jnp.concatenate(split(power), 1)
+    along = lax.broadcasted_iota(jnp.int32, (tile, side), 0) - lax.broadcasted_iota(
+        jnp.int32, (tile, side), 1
+    )
+    across = lax.broadcasted_iota(jnp.int32, (side, tile), 1) - lax.broadcasted_iota(
+        jnp.int32, (side, tile), 0
+    )
+    weight = jnp.zeros((tile, tile), F32)
+    for dc in range(3):
+        for dr in range(3):
+            for s in range(scans):
+                top = near[dc, dr, 2 * s:2 * s + 1, :] + (dr - 1) * tile
+                edge = near[dc, dr, 2 * s + 1:2 * s + 2, :] + (dc - 1) * tile
+                top = jnp.concatenate([top] * (side // top.shape[1]), 1)
+                pick = jnp.where(along == top, 1.0, 0.0).astype(BF16)
+                place = jnp.where(across == edge, 1.0, 0.0).astype(BF16)
+                cut = dot(pick, both)
+                high, low = split(cut[:, :side] + cut[:, side:])
+                weight = weight + (dot(high, place) + dot(low, place))
+    return weight
+
+
+def exchange_kernel(rows, cols, last, scans, obj, probe, near, grad, pgrad, *refs):
     if last:
         obj_out, probe_out, colbuf, mid, rowbuf, new_obj, acc, inbox, res, gsems, rsems, asems = refs
     else:
@@ -163,43 +232,70 @@
     full = grad.shape[1]
     half = (full - tile) // 2
     row, col = lax.axis_index("row"), lax.axis_index("col")
-    orders = stream_orders(rows, cols)
-    greet(rows, cols, orders[0])
-    spots = pgrad.shape[0] // len(orders)
-    plans = [plan(order, spots) for order in orders]
-    los = [s * spots for s in range(len(orders))]
+    groups = phases(rows, cols)
+    greet(rows, cols, groups)
+    spots = pgrad.shape[0] // STREAMS
+    steps = plan(groups, spots)
     box = 0
-    reduces, gathers = [], []
-    for s, steps in enumerate(plans):
-        for step, (axis, bit, count, halves) in enumerate(steps):
-            n = count // 2 if halves else count
-            mine, device = bit_and_partner(axis, bit)
-            lo = los[s]
-            keep = lo + mine * n if halves else lo
-            send = lo + (1 - mine) * n if halves else lo
+    reduces, gathers, ends = {}, {}, []
+    for s in range(STREAMS):
+        lo = s * spots
+        for step, (group, scatters, n) in enumerate(steps):
             source = pgrad if step == 0 else acc
-            buf = inbox.at[pl.ds(box, n)]
-            box += n
-            copy = remote(source.at[pl.ds(send, n)], buf, rsems.at[s], step, device)
-            reduces.append((step, copy, source, keep, n, buf))
-            if halves:
-                span = res.at[pl.ds(keep, n)]
-                gathers.append((s, step, remote(span, span, asems.at[s], step, device)))
-                los[s] = keep
-
-    def start_reduce(at):
-        for step, copy, *_ in reduces:
-            if step == at:
-                copy.start()
-
-    def finish_reduce(at):
-        for step, copy, source, keep, n, buf in reduces:
-            if step == at:
+            _, mine, _ = peer(group, 0)
+            keep = lo + mine * n if scatters else lo
+            copies, spread = [], []
+            for mask in range(1, 1 << len(group)):
+                device, _, theirs = peer(group, mask)
+                send = lo + theirs * n if scatters else lo
+                buf = inbox.at[pl.ds(box, n)]
+                box += n
+                at = (step, mask - 1)
+                copies.append((remote(source.at[pl.ds(send, n)], buf, rsems.at[s], at, device), buf))
+                if scatters:
+                    span = res.at[pl.ds(keep, n)]
+                    spread.append(remote(span, span, asems.at[s], at, device))
+            reduces[s, step] = (copies, source, keep, n)
+            gathers[s, step] = spread
+            lo = keep
+        ends.append(lo)
+    total_steps = len(steps)
+
+    def start_reduce(s, step):
+        for copy, _ in reduces[s, step][0]:
+            copy.start()
+
+    def advance(step):
+        for s in range(STREAMS):
+            copies, source, keep, n = reduces[s, step]
+            for copy, _ in copies:
                 copy.wait()
-                acc[pl.ds(keep, n)] = source[pl.ds(keep, n)] + buf[...]
-
-    total_steps = len(plans[0])
-    start_reduce(0)
+            value = source[pl.ds(keep, n)]
+            for _, buf in copies:
+                value = value + buf[...]
+            if step + 1 < total_steps:
+                acc[pl.ds(keep, n)] = value
+                start_reduce(s, step + 1)
+            else:
+                channels = probe.shape[1]
+                res[pl.ds(keep, n)] = probe[pl.ds(keep, n)] + PROBE_STEP * value[:, :channels] / (
+                    value[:, channels:] + PROBE_REG
+                )
+                start_gather(s, step)
+
+    def start_gather(s, step):
+        for copy in gathers[s, step]:
+            copy.start()
+
+    def back(step):
+        for s in range(STREAMS):
+            for copy in gathers[s, step]:
+                copy.wait()
+            if step:
+                start_gather(s, step - 1)
+
+    for s in range(STREAMS):
+        start_reduce(s, 0)
     by_col = Pair(
         "col", cols, gsems, 0,
         (grad.at[:, :, pl.ds(half + tile, half)], colbuf.at[0]),
@@ -224,16 +320,15 @@
     if not last:
         clear_rim(pad, rows, cols, tile, half)
 
-    finish_reduce(0)
-    start_reduce(1)
+    advance(0)
+    weight = weight_of(probe, near, scans, tile)
     by_col.wait()
     mid[...] = grad[:, :, half:half + tile] + colbuf[0] + colbuf[1]
     by_row.start()
-    finish_reduce(1)
-    start_reduce(2)
+    advance(1)
     by_row.wait()
     total = mid[:, half:half + tile] + rowbuf[0] + rowbuf[1]
-    new = obj[...] + OBJECT_STEP * total[:2] / (total[2:] + OBJECT_REG)
+    new = obj[...] + OBJECT_STEP * total / (weight + OBJECT_REG)
     new_obj[...] = new
     obj_out[...] = new
     if not last:
@@ -241,30 +336,13 @@
         halo_col = col_halo(pad, hsems, 2, cols, tile, half)
         halo_row.start()
         pad[:, pl.ds(half, tile), pl.ds(half, tile)] = new
-    finish_reduce(2)
-    start_reduce(3)
+    for step in range(2, total_steps):
+        advance(step)
     if not last:
         halo_row.wait()
         halo_col.start()
-    for step in range(3, total_steps):
-        finish_reduce(step)
-        if step + 1 < total_steps:
-            start_reduce(step + 1)
-    for s, steps in enumerate(plans):
-        _, _, count, halves = steps[-1]
-        n = count // 2 if halves else count
-        span = pl.ds(los[s], n)
-        terms = acc[span]
-        channels = probe.shape[1]
-        res[span] = probe[span] + PROBE_STEP * terms[:, :channels] / (
-            terms[:, channels:] + PROBE_REG
-        )
-    for at in reversed(range(total_steps)):
-        now = [copy for s, step, copy in gathers if step == at]
-        for copy in now:
-            copy.start()
-        for copy in now:
-            copy.wait()
+    for step in reversed(range(total_steps)):
+        back(step)
     by_col.wait_sent()
     by_row.wait_sent()
     probe_out[...] = res[...]
@@ -275,18 +353,13 @@
         pad_out[...] = pad[...]
 
 
-def exchange(rows, cols, last, obj, probe, grad, pgrad):
+def exchange(rows, cols, last, scans, obj, probe, near, grad, pgrad):
     tile, full = obj.shape[1], grad.shape[1]
     half = (full - tile) // 2
     channels = grad.shape[0]
-    orders = stream_orders(rows, cols)
-    spots = pgrad.shape[0] // len(orders)
-    boxes = sum(
-        count // 2 if halves else count
-        for order in orders
-        for _, _, count, halves in plan(order, spots)
-    )
-    steps = len(orders[0])
+    steps = plan(phases(rows, cols), pgrad.shape[0] // STREAMS)
+    boxes = STREAMS * sum(n * ((1 << len(group)) - 1) for group, _, n in steps)
+    most = max((1 << len(group)) - 1 for group, _, _ in steps)
     vmem = pl.BlockSpec(memory_space=pltpu.VMEM)
     out_shape = [jax.ShapeDtypeStruct(obj.shape, F32), jax.ShapeDtypeStruct(probe.shape, F32)]
     scratch = [
@@ -298,16 +371,16 @@
         pltpu.VMEM((boxes,) + pgrad.shape[1:], F32),
         pltpu.VMEM(probe.shape, F32),
         pltpu.SemaphoreType.DMA((2, 4)),
-        pltpu.SemaphoreType.DMA((len(orders), 2, steps)),
-        pltpu.SemaphoreType.DMA((len(orders), 2, steps)),
+        pltpu.SemaphoreType.DMA((STREAMS, 2, len(steps), most)),
+        pltpu.SemaphoreType.DMA((STREAMS, 2, len(steps), most)),
     ]
     if not last:
         out_shape.append(jax.ShapeDtypeStruct((2, full, full), F32))
         scratch += [pltpu.VMEM((2, full, full), F32), pltpu.SemaphoreType.DMA((2, 4))]
     return pl.pallas_call(
-        lambda *refs: exchange_kernel(rows, cols, last, *refs),
+        lambda *refs: exchange_kernel(rows, cols, last, scans, *refs),
         out_shape=out_shape,
-        in_specs=[vmem] * 4,
+        in_specs=[vmem] * 5,
         out_specs=[vmem] * len(out_shape),
         scratch_shapes=scratch,
         compiler_params=pltpu.CompilerParams(
@@ -315,7 +388,7 @@
             has_side_effects=True,
             vmem_limit_bytes=48 * 1024 * 1024,
         ),
-    )(obj, probe, grad, pgrad)
+    )(obj, probe, near, grad, pgrad)
 
 
 def split_np(table):
@@ -421,11 +494,8 @@
     scans = amp.shape[0]
     probe = {(c, k): whole(tiles, c * modes + k, side) for c in range(2) for k in range(modes)}
     wide[...] = jnp.zeros_like(wide)
-    power = jnp.zeros((side, side), F32)
-    for k in range(modes):
-        power = power + probe[0, k] * probe[0, k] + probe[1, k] * probe[1, k]
     for s in range(scans):
-        row, col = starts[s, 0], starts[s, 1]
+        row, col = starts[s, 0] + side // 2, starts[s, 1] + side // 2
         back_row, back_col = lax.rem(full - row, full), lax.rem(full - col, full)
         win = []
         for ch in range(2):
@@ -454,7 +524,7 @@
                 at = ch * modes + k
                 put(pgrad, at, value, s > 0)
         put(pgrad, 2 * modes, wr * wr + wi * wi, s > 0)
-        for ch, value in enumerate((gr, gi, power)):
+        for ch, value in enumerate((gr, gi)):
             wide[:side, :side] = value
             x = pltpu.roll(pltpu.roll(wide[...], col, 1), row, 0)
             grad[ch] = x if s == 0 else grad[ch] + x
@@ -468,7 +538,7 @@
     return pl.pallas_call(
         step_kernel,
         out_shape=(
-            jax.ShapeDtypeStruct((3, full, full), F32),
+            jax.ShapeDtypeStruct((2, full, full), F32),
             jax.ShapeDtypeStruct((probe.shape[0], probe.shape[1] + 1) + probe.shape[2:], F32),
         ),
         in_specs=[pl.BlockSpec(memory_space=pltpu.SMEM)] + [vmem] * 5,
@@ -483,18 +553,20 @@
     side = probe.shape[2]
     half = side // 2
     rows, cols = lax.axis_size("row"), lax.axis_size("col")
-    starts = offsets[0, 0] + half
+    starts = offsets[0, 0]
+    scans = starts.shape[0]
     measured = amplitudes[0, 0]
     tab = jnp.asarray(tables(side))
     order = jnp.asarray(order_table(side))
     channels = probe.shape[0] * probe.shape[1]
     cut = (channels, side // 8, 8, side // 128, 128)
     tiles = probe.reshape(cut).transpose(3, 1, 0, 2, 4).reshape(-1, channels, 8, 128)
-    padded = halo(rows, cols, object_field, half)
+    offs = jnp.broadcast_to(starts.reshape(-1, 1), (2 * scans, 128))
+    padded, near = halo(rows, cols, object_field, offs, half)
     for iteration in range(ITERS):
         last = iteration + 1 == ITERS
         grad, pgrad = step(starts, padded, tiles, measured, tab, order)
-        out = exchange(rows, cols, last, object_field, tiles, grad, pgrad)
+        out = exchange(rows, cols, last, scans, object_field, tiles, near, grad, pgrad)
         object_field, tiles = out[:2]
         if not last:
             padded = out[2]

time: 139 us -> 116 us (0.83)
  Pallas kernels: 133 us -> 108 us
  local copies, waits for them, and re-layouts: 4.69 us -> 6.68 us
    pallas_call x5, Pallas kernels: 133 us -> 108 us  [the longest x2 78.5 us: exchange(): pl.pallas_call(lambda *refs: exchange_kernel(rows, cols, last, scans, *re...]
    unnamed x11 -> x15, local copies, waits for them, and re-layouts: 2.15 us -> 3.31 us
where the time goes in v2:
time: 116 us
  Pallas kernels  108 us (93%)
  local copies, waits for them, and re-layouts  6.68 us (6%)
    pallas_call x2, Pallas kernels, exchange(): pl.pallas_call(lambda *refs: exchange_kernel(rows, cols, last, scans, *re...  78.5 us
    pallas_call x2, Pallas kernels, step(): pl.pallas_call(step_kernel, out_shape=(jax.ShapeDtypeStruct((2, full, ful...  19.4 us
    pallas_call x1, Pallas kernels, halo(): pl.pallas_call(lambda *refs: halo_kernel(rows, cols, *refs), out_shape=(j...  10.4 us
    unnamed x15, local copies, waits for them, and re-layouts  3.31 us

profile of v2, /device:TPU:0, one launch (start us, length us, event | category | flops | bytes accessed | tf_op | source)
XLA Modules:
  0.0 115.7 jit_solution(18317070079102423904)
XLA Ops:
  0.6 0.0 copy-start.6
  0.6 0.0 copy-start.5
  0.7 0.0 copy-start.4
  0.7 0.0 copy-start.2
  0.7 0.0 copy-start.3
  0.7 0.9 broadcast_in_dim.7
  1.6 0.1 broadcast_in_dim.8.refs_1_
  1.6 1.3 %copy.8 = f32[4,32,8,2,128]{4,2,0,1,3:T(8,128)S(1)} copy(f32[4,32,8,2,128]{4,2,3,1,0:T(8,128)} %bitcast.17) | data formatting | bytes 2097152 | tf_op jit(solution)/shard_map/reshape | solution.py:563
  3.0 0.0 copy-done.2
  3.0 10.4 %shard_map.77 = (f32[2,384,384]{2,1,0:T(8,128)S(1)}, s32[3,3,4,128]{3,2,1,0:T(4,128)S(1)}) custom-call(f32[2,128,128]{2,1,0:T(8,128)S(1)} %copy-done.2, s32[4,128]{1,0:T(4,128)S(1)} %broadcast_in_dim.8.refs_1_), custom_call_target="tpu_custom_call" | custom-call | tf_op jit(solution)/shard_map/pallas_call | solution.py:177
  13.5 0.0 copy-done.6
  13.5 0.0 copy-done.5
  13.5 0.0 copy-done.4
  13.5 0.0 copy-done.3
  13.5 9.7 %shard_map.78 = (f32[2,384,384]{2,1,0:T(8,128)S(1)}, f32[64,5,8,128]{3,2,1,0:T(8,128)}) custom-call(s32[2,2]{1,0:T(2,128)S(1)} %bitcast.15, f32[2,384,384]{2,1,0:T(8,128)S(1)} %get-tuple-element.14.obj, f32[64,4,8,128]{3,2,1,0:T(8,128)S(1)} %bitcast.10, f32[2,256,256]{2,1,0:T(8,128)S(1)} %bitcast.13, bf16[8,256,256]{2,1,0:T(8,128)(2,1)S(1)} %copy-done.5, ...), custom_call_target="tpu_custom_call" | custom-call | flops 3221225472 | bytes 6291456 | tf_op jit(solution)/shard_map/pallas_call | solution.py:538
  23.2 0.0 copy-start.1
  23.2 1.3 %copy-done.1 = f32[64,5,8,128]{3,2,1,0:T(8,128)S(1)} copy-done((f32[64,5,8,128]{3,2,1,0:T(8,128)S(1)}, f32[64,5,8,128]{3,2,1,0:T(8,128)}, u32[]{:S(2)}) %copy-start.1) | copy-done | bytes 1310744
  24.5 46.2 %shard_map.79 = (f32[2,128,128]{2,1,0:T(8,128)S(1)}, f32[64,4,8,128]{3,2,1,0:T(8,128)S(1)}, f32[2,384,384]{2,1,0:T(8,128)S(1)}) custom-call(f32[2,128,128]{2,1,0:T(8,128)S(1)} %copy-done.2, f32[64,4,8,128]{3,2,1,0:T(8,128)S(1)} %bitcast.11, s32[3,3,4,128]{3,2,1,0:T(4,128)S(1)} %get-tuple-element.13.refs_2_, f32[2,384,384]{2,1,0:T(8,128)S(1)} %get-tuple-element.15.refs_3_, ...), custom_call_target="tpu_custom_call" | custom-call | tf_op jit(solution)/shard_map/pallas_call | solution.py:380
  70.6 9.7 %shard_map.80 = (f32[2,384,384]{2,1,0:T(8,128)S(1)}, f32[64,5,8,128]{3,2,1,0:T(8,128)}) custom-call(s32[2,2]{1,0:T(2,128)S(1)} %bitcast.16, f32[2,384,384]{2,1,0:T(8,128)S(1)} %get-tuple-element.19.obj, f32[64,4,8,128]{3,2,1,0:T(8,128)S(1)} %get-tuple-element.18.tiles.refs_1_, f32[2,256,256]{2,1,0:T(8,128)S(1)} %bitcast.14, ...), custom_call_target="tpu_custom_call" | custom-call | flops 3221225472 | bytes 6291456 | tf_op jit(solution)/shard_map/pallas_call | solution.py:538
  80.3 0.0 copy-start
  80.3 1.3 %copy-done = f32[64,5,8,128]{3,2,1,0:T(8,128)S(1)} copy-done((f32[64,5,8,128]{3,2,1,0:T(8,128)S(1)}, f32[64,5,8,128]{3,2,1,0:T(8,128)}, u32[]{:S(2)}) %copy-start) | copy-done | bytes 1310744
  81.6 32.3 %shard_map.81 = (f32[2,128,128]{2,1,0:T(8,128)S(1)}, f32[64,4,8,128]{3,2,1,0:T(8,128)S(1)}) custom-call(f32[2,128,128]{2,1,0:T(8,128)S(1)} %get-tuple-element.17.refs_0_, f32[64,4,8,128]{3,2,1,0:T(8,128)S(1)} %get-tuple-element.18.tiles.refs_1_, s32[3,3,4,128]{3,2,1,0:T(4,128)S(1)} %get-tuple-element.13.refs_2_, ...), custom_call_target="tpu_custom_call" | custom-call | tf_op jit(solution)/shard_map/pallas_call | solution.py:380
  114.0 1.1 copy.9
  115.0 0.7 copy.11
Async XLA Ops:
  0.6 12.8 %copy-start.6 = (bf16[2,256,256]{2,1,0:T(8,128)(2,1)S(1)}, bf16[2,256,256]{2,1,0:T(8,128)(2,1)}, u32[]{:S(2)}) copy-start(bf16[2,256,256]{2,1,0:T(8,128)(2,1)} %constant.5.clone.order) | copy-start | bytes 786436
  0.6 12.8 %copy-start.5 = (bf16[8,256,256]{2,1,0:T(8,128)(2,1)S(1)}, bf16[8,256,256]{2,1,0:T(8,128)(2,1)}, u32[]{:S(2)}) copy-start(bf16[8,256,256]{2,1,0:T(8,128)(2,1)} %constant.4.clone.tab) | copy-start | bytes 3145732
  0.7 12.8 %copy-start.4 = (s32[1,1,2,2]{3,2,1,0:T(2,128)S(1)}, s32[1,1,2,2]{3,2,1,0:T(2,128)}, u32[]{:S(2)}) copy-start(s32[1,1,2,2]{3,2,1,0:T(2,128)} %param.9) | copy-start | bytes 52
  0.7 2.3 %copy-start.2 = (f32[2,128,128]{2,1,0:T(8,128)S(1)}, f32[2,128,128]{2,1,0:T(8,128)}, u32[]{:S(2)}) copy-start(f32[2,128,128]{2,1,0:T(8,128)} %refs_0_.3) | copy-start | bytes 393220
  0.7 12.8 %copy-start.3 = (f32[1,1,2,256,256]{4,3,2,1,0:T(8,128)S(1)}, f32[1,1,2,256,256]{4,3,2,1,0:T(8,128)}, u32[]{:S(2)}) copy-start(f32[1,1,2,256,256]{4,3,2,1,0:T(8,128)} %param.8) | copy-start | bytes 1572868
  23.2 1.3 %copy-start.1 = (f32[64,5,8,128]{3,2,1,0:T(8,128)S(1)}, f32[64,5,8,128]{3,2,1,0:T(8,128)}, u32[]{:S(2)}) copy-start(f32[64,5,8,128]{3,2,1,0:T(8,128)} %get-tuple-element.16.refs_4_) | copy-start | bytes 3932164
  80.3 1.3 %copy-start = (f32[64,5,8,128]{3,2,1,0:T(8,128)S(1)}, f32[64,5,8,128]{3,2,1,0:T(8,128)}, u32[]{:S(2)}) copy-start(f32[64,5,8,128]{3,2,1,0:T(8,128)} %get-tuple-element.21.refs_4_) | copy-start | bytes 3932164

commit v3 on v2

--- a/solution.py
+++ b/solution.py
@@ -31,8 +31,11 @@
 def phases(rows, cols):
     row_bits, col_bits = bits_of("row", rows), bits_of("col", cols)
     rest = row_bits[1:] + col_bits[2:]
-    groups = [col_bits[:1], col_bits[1:2] + row_bits[:1]]
-    return groups + [rest[i:i + 2] for i in range(0, len(rest), 2)]
+    first, near = col_bits[:1], col_bits[1:2] + row_bits[:1]
+    one = [first, near] + [rest[i:i + 2] for i in range(0, len(rest), 2)]
+    late = rest[1:]
+    two = [first, rest[:1], near] + [late[i:i + 2] for i in range(0, len(late), 2)]
+    return [one, two]
 
 
 def plan(groups, count):
@@ -74,8 +77,13 @@
         {"row": lax.rem(row + 1, rows)}, {"row": lax.rem(row + rows - 1, rows)},
         {"col": lax.rem(col + 1, cols)}, {"col": lax.rem(col + cols - 1, cols)},
     ]
+    known = []
     for group in groups:
-        devices += [peer(group, mask)[0] for mask in range(1, 1 << len(group))]
+        for mask in range(1, 1 << len(group)):
+            flipped = sorted(item for i, item in enumerate(group) if mask >> i & 1)
+            if flipped not in known:
+                known.append(flipped)
+                devices.append(peer(group, mask)[0])
     for device in devices:
         pl.semaphore_signal(barrier, inc=1, device_id=device, device_id_type=MESH)
     pl.semaphore_wait(barrier, len(devices))
@@ -135,7 +143,7 @@
     pl.when(col == cols - 1)(clear(every, every, pl.ds(half + tile, half)))
 
 
-def halo_kernel(rows, cols, obj, offs, out, near_out, pad, near, sems):
+def halo_kernel(rows, cols, obj, offs, probe, out, near_out, tiles, pad, near, sems):
     tile = obj.shape[1]
     half = (pad.shape[1] - tile) // 2
     greet(rows, cols, ())
@@ -157,6 +165,8 @@
     pl.when(col == cols - 1)(absent(2))
     clear_rim(pad, rows, cols, tile, half)
     pad[:, pl.ds(half, tile), pl.ds(half, tile)] = obj[...]
+    for at in range(probe.shape[0]):
+        put(tiles, at, probe[at], False)
     by_row.wait()
     by_col = col_halo(pad, sems, 2, cols, tile, half)
     by_col.start()
@@ -171,7 +181,7 @@
     near_out[...] = near[...]
 
 
-def halo(rows, cols, obj, offs, half):
+def halo(rows, cols, obj, offs, probe, half):
     full = obj.shape[1] + 2 * half
     vmem = pl.BlockSpec(memory_space=pltpu.VMEM)
     return pl.pallas_call(
@@ -179,9 +189,10 @@
         out_shape=(
             jax.ShapeDtypeStruct((2, full, full), F32),
             jax.ShapeDtypeStruct((3, 3) + offs.shape, jnp.int32),
+            jax.ShapeDtypeStruct((probe[0].size // 1024, probe.shape[0], 8, 128), F32),
         ),
-        in_specs=[vmem, vmem],
-        out_specs=(vmem, vmem),
+        in_specs=[vmem, vmem, vmem],
+        out_specs=(vmem, vmem, vmem),
         scratch_shapes=[
             pltpu.VMEM((2, full, full), F32),
             pltpu.VMEM((3, 3) + offs.shape, jnp.int32),
@@ -190,7 +201,7 @@
         compiler_params=pltpu.CompilerParams(
             collective_id=0, has_side_effects=True, vmem_limit_bytes=32 * 1024 * 1024
         ),
-    )(obj, offs)
+    )(obj, offs, probe)
 
 
 def weight_of(probe, near, scans, tile):
@@ -233,14 +244,14 @@
     half = (full - tile) // 2
     row, col = lax.axis_index("row"), lax.axis_index("col")
     groups = phases(rows, cols)
-    greet(rows, cols, groups)
+    greet(rows, cols, [group for stream in groups for group in stream])
     spots = pgrad.shape[0] // STREAMS
-    steps = plan(groups, spots)
+    plans = [plan(group, spots) for group in groups]
     box = 0
     reduces, gathers, ends = {}, {}, []
     for s in range(STREAMS):
         lo = s * spots
-        for step, (group, scatters, n) in enumerate(steps):
+        for step, (group, scatters, n) in enumerate(plans[s]):
             source = pgrad if step == 0 else acc
             _, mine, _ = peer(group, 0)
             keep = lo + mine * n if scatters else lo
@@ -259,7 +270,7 @@
             gathers[s, step] = spread
             lo = keep
         ends.append(lo)
-    total_steps = len(steps)
+    most = max(len(steps) for steps in plans)
 
     def start_reduce(s, step):
         for copy, _ in reduces[s, step][0]:
@@ -267,13 +278,15 @@
 
     def advance(step):
         for s in range(STREAMS):
+            if step >= len(plans[s]):
+                continue
             copies, source, keep, n = reduces[s, step]
             for copy, _ in copies:
                 copy.wait()
             value = source[pl.ds(keep, n)]
             for _, buf in copies:
                 value = value + buf[...]
-            if step + 1 < total_steps:
+            if step + 1 < len(plans[s]):
                 acc[pl.ds(keep, n)] = value
                 start_reduce(s, step + 1)
             else:
@@ -287,8 +300,11 @@
         for copy in gathers[s, step]:
             copy.start()
 
-    def back(step):
+    def back(turn):
         for s in range(STREAMS):
+            step = len(plans[s]) - 1 - turn
+            if step < 0:
+                continue
             for copy in gathers[s, step]:
                 copy.wait()
             if step:
@@ -336,13 +352,13 @@
         halo_col = col_halo(pad, hsems, 2, cols, tile, half)
         halo_row.start()
         pad[:, pl.ds(half, tile), pl.ds(half, tile)] = new
-    for step in range(2, total_steps):
+    for step in range(2, most):
         advance(step)
     if not last:
         halo_row.wait()
         halo_col.start()
-    for step in reversed(range(total_steps)):
-        back(step)
+    for turn in range(most):
+        back(turn)
     by_col.wait_sent()
     by_row.wait_sent()
     probe_out[...] = res[...]
@@ -357,9 +373,10 @@
     tile, full = obj.shape[1], grad.shape[1]
     half = (full - tile) // 2
     channels = grad.shape[0]
-    steps = plan(phases(rows, cols), pgrad.shape[0] // STREAMS)
-    boxes = STREAMS * sum(n * ((1 << len(group)) - 1) for group, _, n in steps)
-    most = max((1 << len(group)) - 1 for group, _, _ in steps)
+    plans = [plan(groups, pgrad.shape[0] // STREAMS) for groups in phases(rows, cols)]
+    boxes = sum(n * ((1 << len(group)) - 1) for steps in plans for group, _, n in steps)
+    most = max((1 << len(group)) - 1 for steps in plans for group, _, _ in steps)
+    longest = max(len(steps) for steps in plans)
     vmem = pl.BlockSpec(memory_space=pltpu.VMEM)
     out_shape = [jax.ShapeDtypeStruct(obj.shape, F32), jax.ShapeDtypeStruct(probe.shape, F32)]
     scratch = [
@@ -371,8 +388,8 @@
         pltpu.VMEM((boxes,) + pgrad.shape[1:], F32),
         pltpu.VMEM(probe.shape, F32),
         pltpu.SemaphoreType.DMA((2, 4)),
-        pltpu.SemaphoreType.DMA((STREAMS, 2, len(steps), most)),
-        pltpu.SemaphoreType.DMA((STREAMS, 2, len(steps), most)),
+        pltpu.SemaphoreType.DMA((STREAMS, 2, longest, most)),
+        pltpu.SemaphoreType.DMA((STREAMS, 2, longest, most)),
     ]
     if not last:
         out_shape.append(jax.ShapeDtypeStruct((2, full, full), F32))
@@ -559,10 +576,9 @@
     tab = jnp.asarray(tables(side))
     order = jnp.asarray(order_table(side))
     channels = probe.shape[0] * probe.shape[1]
-    cut = (channels, side // 8, 8, side // 128, 128)
-    tiles = probe.reshape(cut).transpose(3, 1, 0, 2, 4).reshape(-1, channels, 8, 128)
     offs = jnp.broadcast_to(starts.reshape(-1, 1), (2 * scans, 128))
-    padded, near = halo(rows, cols, object_field, offs, half)
+    modes = probe.reshape(channels, side, side)
+    padded, near, tiles = halo(rows, cols, object_field, offs, modes, half)
     for iteration in range(ITERS):
         last = iteration + 1 == ITERS
         grad, pgrad = step(starts, padded, tiles, measured, tab, order)

time: 116 us -> 122 us (1.052)
  Pallas kernels: 108 us -> 112 us
  local copies, waits for them, and re-layouts: 6.68 us -> 8.61 us
    pallas_call x2, Pallas kernels: 78.5 us -> 82.5 us  [exchange(): pl.pallas_call(lambda *refs: exchange_kernel(rows, cols, last, scans, *re...]
    unnamed x15 -> x21, local copies, waits for them, and re-layouts: 3.31 us -> 6.65 us
    reshape x1 -> x0, local copies, waits for them, and re-layouts: 1.35 us -> none  [local(): probe.reshape(cut).transpose(3, 1, 0, 2, 4).reshape(-1, channels, 8, 128)]
where the time goes in v3:
time: 122 us; the launch traced here: 121 us
  Pallas kernels  112 us (92%)
  local copies, waits for them, and re-layouts  8.61 us (7%)
    pallas_call x2, Pallas kernels, exchange(): pl.pallas_call(lambda *refs: exchange_kernel(rows, cols, last, scans, *re...  82.5 us
    pallas_call x2, Pallas kernels, step(): pl.pallas_call(step_kernel, out_shape=(jax.ShapeDtypeStruct((2, full, ful...  19.2 us
    pallas_call x1, Pallas kernels, halo(): pl.pallas_call(lambda *refs: halo_kernel(rows, cols, *refs), out_shape=(j...  10.4 us
    unnamed x21, local copies, waits for them, and re-layouts  6.65 us

profile of v3, /device:TPU:0, one launch (start us, length us, event | category | flops | bytes accessed | tf_op | source)
XLA Modules:
  0.0 121.5 jit_solution(2256472190122789052)
XLA Ops:
  0.6 0.0 copy-start.6
  0.6 0.8 broadcast_in_dim.7
  1.5 0.1 broadcast_in_dim.8.refs_1_
  1.5 0.0 copy-start.2
  1.5 1.2 %copy-done.2 = f32[2,2,256,256]{3,2,1,0:T(8,128)S(1)} copy-done((f32[2,2,256,256]{3,2,1,0:T(8,128)S(1)}, f32[2,2,256,256]{3,2,1,0:T(8,128)}, u32[]{:S(2)}) %copy-start.2) | copy-done | bytes 1048600
  2.8 0.0 copy-start.3
  2.8 0.9 copy-done.3
  3.7 0.0 copy-start.5
  3.7 0.0 copy-start.9
  3.7 10.4 %shard_map.77 = (f32[2,384,384]{2,1,0:T(8,128)S(1)}, s32[3,3,4,128]{3,2,1,0:T(4,128)S(1)}, f32[64,4,8,128]{3,2,1,0:T(8,128)S(1)}) custom-call(f32[2,128,128]{2,1,0:T(8,128)S(1)} %copy-done.3, s32[4,128]{1,0:T(4,128)S(1)} %broadcast_in_dim.8.refs_1_, f32[4,256,256]{2,1,0:T(8,128)S(1)} %bitcast.7), custom_call_target="tpu_custom_call" | custom-call | tf_op jit(solution)/shard_map/pallas_call | solution.py:187
  14.1 0.0 copy-done.6
  14.1 0.0 copy-done.5
  14.1 0.0 copy-done.9
  14.1 0.0 copy-start.7
  14.1 1.2 %copy-done.7 = bf16[8,256,256]{2,1,0:T(8,128)(2,1)S(1)} copy-done((bf16[8,256,256]{2,1,0:T(8,128)(2,1)S(1)}, bf16[8,256,256]{2,1,0:T(8,128)(2,1)}, u32[]{:S(2)}) %copy-start.7) | copy-done | bytes 1048600
  15.3 0.0 copy-start.4
  15.3 9.7 %shard_map.78 = (f32[2,384,384]{2,1,0:T(8,128)S(1)}, f32[64,5,8,128]{3,2,1,0:T(8,128)}) custom-call(s32[2,2]{1,0:T(2,128)S(1)} %bitcast.11, f32[2,384,384]{2,1,0:T(8,128)S(1)} %get-tuple-element.16.obj, f32[64,4,8,128]{3,2,1,0:T(8,128)S(1)} %get-tuple-element.14.tiles.refs_1_, f32[2,256,256]{2,1,0:T(8,128)S(1)} %bitcast.9, ...), custom_call_target="tpu_custom_call" | custom-call | flops 3221225472 | bytes 6291456 | tf_op jit(solution)/shard_map/pallas_call | solution.py:555
  25.0 0.0 copy-done.4
  25.0 0.0 copy-start.1
  25.0 1.3 %copy-done.1 = f32[64,5,8,128]{3,2,1,0:T(8,128)S(1)} copy-done((f32[64,5,8,128]{3,2,1,0:T(8,128)S(1)}, f32[64,5,8,128]{3,2,1,0:T(8,128)}, u32[]{:S(2)}) %copy-start.1) | copy-done | bytes 1310744
  26.4 0.0 copy-start.8
  26.4 48.8 %shard_map.79 = (f32[2,128,128]{2,1,0:T(8,128)S(1)}, f32[64,4,8,128]{3,2,1,0:T(8,128)S(1)}, f32[2,384,384]{2,1,0:T(8,128)S(1)}) custom-call(f32[2,128,128]{2,1,0:T(8,128)S(1)} %copy-done.4, f32[64,4,8,128]{3,2,1,0:T(8,128)S(1)} %get-tuple-element.14.tiles.refs_1_, s32[3,3,4,128]{3,2,1,0:T(4,128)S(1)} %get-tuple-element.15.refs_2_, ...), custom_call_target="tpu_custom_call" | custom-call | tf_op jit(solution)/shard_map/pallas_call | solution.py:397
  75.1 0.0 copy-done.8
  75.1 9.6 %shard_map.80 = (f32[2,384,384]{2,1,0:T(8,128)S(1)}, f32[64,5,8,128]{3,2,1,0:T(8,128)}) custom-call(s32[2,2]{1,0:T(2,128)S(1)} %bitcast.12, f32[2,384,384]{2,1,0:T(8,128)S(1)} %get-tuple-element.21.obj, f32[64,4,8,128]{3,2,1,0:T(8,128)S(1)} %get-tuple-element.20.tiles.refs_1_, f32[2,256,256]{2,1,0:T(8,128)S(1)} %bitcast.10, ...), custom_call_target="tpu_custom_call" | custom-call | flops 3221225472 | bytes 6291456 | tf_op jit(solution)/shard_map/pallas_call | solution.py:555
  84.7 0.0 copy-start
  84.7 1.3 %copy-done = f32[64,5,8,128]{3,2,1,0:T(8,128)S(1)} copy-done((f32[64,5,8,128]{3,2,1,0:T(8,128)S(1)}, f32[64,5,8,128]{3,2,1,0:T(8,128)}, u32[]{:S(2)}) %copy-start) | copy-done | bytes 1310744
  86.0 33.8 %shard_map.81 = (f32[2,128,128]{2,1,0:T(8,128)S(1)}, f32[64,4,8,128]{3,2,1,0:T(8,128)S(1)}) custom-call(f32[2,128,128]{2,1,0:T(8,128)S(1)} %get-tuple-element.19.refs_0_, f32[64,4,8,128]{3,2,1,0:T(8,128)S(1)} %get-tuple-element.20.tiles.refs_1_, s32[3,3,4,128]{3,2,1,0:T(4,128)S(1)} %get-tuple-element.15.refs_2_, ...), custom_call_target="tpu_custom_call" | custom-call | tf_op jit(solution)/shard_map/pallas_call | solution.py:397
  119.8 1.1 copy.8
  120.8 0.7 copy.10
Async XLA Ops:
  0.6 13.5 %copy-start.6 = (s32[1,1,2,2]{3,2,1,0:T(2,128)S(1)}, s32[1,1,2,2]{3,2,1,0:T(2,128)}, u32[]{:S(2)}) copy-start(s32[1,1,2,2]{3,2,1,0:T(2,128)} %param.9) | copy-start | bytes 52
  1.5 1.2 %copy-start.2 = (f32[2,2,256,256]{3,2,1,0:T(8,128)S(1)}, f32[2,2,256,256]{3,2,1,0:T(8,128)}, u32[]{:S(2)}) copy-start(f32[2,2,256,256]{3,2,1,0:T(8,128)} %param.7) | copy-start | bytes 3145732
  2.8 0.9 copy-start.3
  3.7 10.4 %copy-start.5 = (f32[1,1,2,256,256]{4,3,2,1,0:T(8,128)S(1)}, f32[1,1,2,256,256]{4,3,2,1,0:T(8,128)}, u32[]{:S(2)}) copy-start(f32[1,1,2,256,256]{4,3,2,1,0:T(8,128)} %param.8) | copy-start | bytes 1572868
  3.7 10.4 %copy-start.9 = (bf16[2,256,256]{2,1,0:T(8,128)(2,1)S(1)}, bf16[2,256,256]{2,1,0:T(8,128)(2,1)}, u32[]{:S(2)}) copy-start(bf16[2,256,256]{2,1,0:T(8,128)(2,1)} %constant.5.clone.order) | copy-start | bytes 786436
  14.1 1.2 %copy-start.7 = (bf16[8,256,256]{2,1,0:T(8,128)(2,1)S(1)}, bf16[8,256,256]{2,1,0:T(8,128)(2,1)}, u32[]{:S(2)}) copy-start(bf16[8,256,256]{2,1,0:T(8,128)(2,1)} %constant.4.clone.tab) | copy-start | bytes 3145732
  15.3 9.7 %copy-start.4 = (f32[2,128,128]{2,1,0:T(8,128)S(1)}, f32[2,128,128]{2,1,0:T(8,128)}, u32[]{:S(2)}) copy-start(f32[2,128,128]{2,1,0:T(8,128)} %refs_0_.3) | copy-start | bytes 393220
  25.0 1.3 %copy-start.1 = (f32[64,5,8,128]{3,2,1,0:T(8,128)S(1)}, f32[64,5,8,128]{3,2,1,0:T(8,128)}, u32[]{:S(2)}) copy-start(f32[64,5,8,128]{3,2,1,0:T(8,128)} %get-tuple-element.18.refs_4_) | copy-start | bytes 3932164
  26.4 48.8 %copy-start.8 = (bf16[8,256,256]{2,1,0:T(8,128)(2,1)S(1)}, bf16[8,256,256]{2,1,0:T(8,128)(2,1)}, u32[]{:S(2)}) copy-start(bf16[8,256,256]{2,1,0:T(8,128)(2,1)} %constant.4.clone.tab) | copy-start | bytes 3145732
  84.7 1.3 %copy-start = (f32[64,5,8,128]{3,2,1,0:T(8,128)S(1)}, f32[64,5,8,128]{3,2,1,0:T(8,128)}, u32[]{:S(2)}) copy-start(f32[64,5,8,128]{3,2,1,0:T(8,128)} %get-tuple-element.23.refs_4_) | copy-start | bytes 3932164

commit v4 on v2

--- a/solution.py
+++ b/solution.py
@@ -294,8 +294,6 @@
             if step:
                 start_gather(s, step - 1)
 
-    for s in range(STREAMS):
-        start_reduce(s, 0)
     by_col = Pair(
         "col", cols, gsems, 0,
         (grad.at[:, :, pl.ds(half + tile, half)], colbuf.at[0]),
@@ -307,6 +305,8 @@
         (mid.at[:, pl.ds(0, half)], rowbuf.at[1]),
     )
     by_col.start()
+    for s in range(STREAMS):
+        start_reduce(s, 0)
 
     def clear(ref, at):
         def run():
@@ -321,10 +321,10 @@
         clear_rim(pad, rows, cols, tile, half)
 
     advance(0)
-    weight = weight_of(probe, near, scans, tile)
     by_col.wait()
     mid[...] = grad[:, :, half:half + tile] + colbuf[0] + colbuf[1]
     by_row.start()
+    weight = weight_of(probe, near, scans, tile)
     advance(1)
     by_row.wait()
     total = mid[:, half:half + tile] + rowbuf[0] + rowbuf[1]

time: 116 us -> 117 us (level)
  no operation moved by 1% of the time
where the time goes in v4:
time: 117 us
  Pallas kernels  109 us (93%)
  local copies, waits for them, and re-layouts  6.68 us (6%)
    pallas_call x2, Pallas kernels, exchange(): pl.pallas_call(lambda *refs: exchange_kernel(rows, cols, last, scans, *re...  79.5 us
    pallas_call x2, Pallas kernels, step(): pl.pallas_call(step_kernel, out_shape=(jax.ShapeDtypeStruct((2, full, ful...  19.4 us
    pallas_call x1, Pallas kernels, halo(): pl.pallas_call(lambda *refs: halo_kernel(rows, cols, *refs), out_shape=(j...  10.4 us
    unnamed x15, local copies, waits for them, and re-layouts  3.31 us

profile of v4, /device:TPU:0, one launch (start us, length us, event | category | flops | bytes accessed | tf_op | source)
XLA Modules:
  0.0 116.7 jit_solution(312129280445293388)
XLA Ops:
  0.6 0.0 copy-start.6
  0.6 0.0 copy-start.5
  0.7 0.0 copy-start.4
  0.7 0.0 copy-start.2
  0.7 0.0 copy-start.3
  0.7 0.9 broadcast_in_dim.7
  1.6 0.1 broadcast_in_dim.8.refs_1_
  1.6 1.3 %copy.8 = f32[4,32,8,2,128]{4,2,0,1,3:T(8,128)S(1)} copy(f32[4,32,8,2,128]{4,2,3,1,0:T(8,128)} %bitcast.17) | data formatting | bytes 2097152 | tf_op jit(solution)/shard_map/reshape | solution.py:563
  3.0 0.0 copy-done.2
  3.0 10.4 %shard_map.77 = (f32[2,384,384]{2,1,0:T(8,128)S(1)}, s32[3,3,4,128]{3,2,1,0:T(4,128)S(1)}) custom-call(f32[2,128,128]{2,1,0:T(8,128)S(1)} %copy-done.2, s32[4,128]{1,0:T(4,128)S(1)} %broadcast_in_dim.8.refs_1_), custom_call_target="tpu_custom_call" | custom-call | tf_op jit(solution)/shard_map/pallas_call | solution.py:177
  13.5 0.0 copy-done.6
  13.5 0.0 copy-done.5
  13.5 0.0 copy-done.4
  13.5 0.0 copy-done.3
  13.5 9.7 %shard_map.78 = (f32[2,384,384]{2,1,0:T(8,128)S(1)}, f32[64,5,8,128]{3,2,1,0:T(8,128)}) custom-call(s32[2,2]{1,0:T(2,128)S(1)} %bitcast.15, f32[2,384,384]{2,1,0:T(8,128)S(1)} %get-tuple-element.14.obj, f32[64,4,8,128]{3,2,1,0:T(8,128)S(1)} %bitcast.10, f32[2,256,256]{2,1,0:T(8,128)S(1)} %bitcast.13, bf16[8,256,256]{2,1,0:T(8,128)(2,1)S(1)} %copy-done.5, ...), custom_call_target="tpu_custom_call" | custom-call | flops 3221225472 | bytes 6291456 | tf_op jit(solution)/shard_map/pallas_call | solution.py:538
  23.2 0.0 copy-start.1
  23.2 1.3 %copy-done.1 = f32[64,5,8,128]{3,2,1,0:T(8,128)S(1)} copy-done((f32[64,5,8,128]{3,2,1,0:T(8,128)S(1)}, f32[64,5,8,128]{3,2,1,0:T(8,128)}, u32[]{:S(2)}) %copy-start.1) | copy-done | bytes 1310744
  24.5 47.1 %shard_map.79 = (f32[2,128,128]{2,1,0:T(8,128)S(1)}, f32[64,4,8,128]{3,2,1,0:T(8,128)S(1)}, f32[2,384,384]{2,1,0:T(8,128)S(1)}) custom-call(f32[2,128,128]{2,1,0:T(8,128)S(1)} %copy-done.2, f32[64,4,8,128]{3,2,1,0:T(8,128)S(1)} %bitcast.11, s32[3,3,4,128]{3,2,1,0:T(4,128)S(1)} %get-tuple-element.13.refs_2_, f32[2,384,384]{2,1,0:T(8,128)S(1)} %get-tuple-element.15.refs_3_, ...), custom_call_target="tpu_custom_call" | custom-call | tf_op jit(solution)/shard_map/pallas_call | solution.py:380
  71.5 9.7 %shard_map.80 = (f32[2,384,384]{2,1,0:T(8,128)S(1)}, f32[64,5,8,128]{3,2,1,0:T(8,128)}) custom-call(s32[2,2]{1,0:T(2,128)S(1)} %bitcast.16, f32[2,384,384]{2,1,0:T(8,128)S(1)} %get-tuple-element.19.obj, f32[64,4,8,128]{3,2,1,0:T(8,128)S(1)} %get-tuple-element.18.tiles.refs_1_, f32[2,256,256]{2,1,0:T(8,128)S(1)} %bitcast.14, ...), custom_call_target="tpu_custom_call" | custom-call | flops 3221225472 | bytes 6291456 | tf_op jit(solution)/shard_map/pallas_call | solution.py:538
  81.2 0.0 copy-start
  81.2 1.3 %copy-done = f32[64,5,8,128]{3,2,1,0:T(8,128)S(1)} copy-done((f32[64,5,8,128]{3,2,1,0:T(8,128)S(1)}, f32[64,5,8,128]{3,2,1,0:T(8,128)}, u32[]{:S(2)}) %copy-start) | copy-done | bytes 1310744
  82.5 32.5 %shard_map.81 = (f32[2,128,128]{2,1,0:T(8,128)S(1)}, f32[64,4,8,128]{3,2,1,0:T(8,128)S(1)}) custom-call(f32[2,128,128]{2,1,0:T(8,128)S(1)} %get-tuple-element.17.refs_0_, f32[64,4,8,128]{3,2,1,0:T(8,128)S(1)} %get-tuple-element.18.tiles.refs_1_, s32[3,3,4,128]{3,2,1,0:T(4,128)S(1)} %get-tuple-element.13.refs_2_, ...), custom_call_target="tpu_custom_call" | custom-call | tf_op jit(solution)/shard_map/pallas_call | solution.py:380
  115.0 1.1 copy.9
  116.1 0.7 copy.11
Async XLA Ops:
  0.6 12.8 %copy-start.6 = (bf16[2,256,256]{2,1,0:T(8,128)(2,1)S(1)}, bf16[2,256,256]{2,1,0:T(8,128)(2,1)}, u32[]{:S(2)}) copy-start(bf16[2,256,256]{2,1,0:T(8,128)(2,1)} %constant.5.clone.order) | copy-start | bytes 786436
  0.6 12.8 %copy-start.5 = (bf16[8,256,256]{2,1,0:T(8,128)(2,1)S(1)}, bf16[8,256,256]{2,1,0:T(8,128)(2,1)}, u32[]{:S(2)}) copy-start(bf16[8,256,256]{2,1,0:T(8,128)(2,1)} %constant.4.clone.tab) | copy-start | bytes 3145732
  0.7 12.8 %copy-start.4 = (s32[1,1,2,2]{3,2,1,0:T(2,128)S(1)}, s32[1,1,2,2]{3,2,1,0:T(2,128)}, u32[]{:S(2)}) copy-start(s32[1,1,2,2]{3,2,1,0:T(2,128)} %param.9) | copy-start | bytes 52
  0.7 2.3 %copy-start.2 = (f32[2,128,128]{2,1,0:T(8,128)S(1)}, f32[2,128,128]{2,1,0:T(8,128)}, u32[]{:S(2)}) copy-start(f32[2,128,128]{2,1,0:T(8,128)} %refs_0_.3) | copy-start | bytes 393220
  0.7 12.8 %copy-start.3 = (f32[1,1,2,256,256]{4,3,2,1,0:T(8,128)S(1)}, f32[1,1,2,256,256]{4,3,2,1,0:T(8,128)}, u32[]{:S(2)}) copy-start(f32[1,1,2,256,256]{4,3,2,1,0:T(8,128)} %param.8) | copy-start | bytes 1572868
  23.2 1.3 %copy-start.1 = (f32[64,5,8,128]{3,2,1,0:T(8,128)S(1)}, f32[64,5,8,128]{3,2,1,0:T(8,128)}, u32[]{:S(2)}) copy-start(f32[64,5,8,128]{3,2,1,0:T(8,128)} %get-tuple-element.16.refs_4_) | copy-start | bytes 3932164
  81.2 1.3 %copy-start = (f32[64,5,8,128]{3,2,1,0:T(8,128)S(1)}, f32[64,5,8,128]{3,2,1,0:T(8,128)}, u32[]{:S(2)}) copy-start(f32[64,5,8,128]{3,2,1,0:T(8,128)} %get-tuple-element.21.refs_4_) | copy-start | bytes 3932164

commit v5 on v2

--- a/solution.py
+++ b/solution.py
@@ -325,7 +325,8 @@
     by_col.wait()
     mid[...] = grad[:, :, half:half + tile] + colbuf[0] + colbuf[1]
     by_row.start()
-    advance(1)
+    if last:
+        advance(1)
     by_row.wait()
     total = mid[:, half:half + tile] + rowbuf[0] + rowbuf[1]
     new = obj[...] + OBJECT_STEP * total / (weight + OBJECT_REG)
@@ -336,11 +337,11 @@
         halo_col = col_halo(pad, hsems, 2, cols, tile, half)
         halo_row.start()
         pad[:, pl.ds(half, tile), pl.ds(half, tile)] = new
+        advance(1)
+        halo_row.wait()
+        halo_col.start()
     for step in range(2, total_steps):
         advance(step)
-    if not last:
-        halo_row.wait()
-        halo_col.start()
     for step in reversed(range(total_steps)):
         back(step)
     by_col.wait_sent()

time: 116 us -> 117 us (level)
  no operation moved by 1% of the time
where the time goes in v5:
time: 117 us
  Pallas kernels  109 us (93%)
  local copies, waits for them, and re-layouts  6.68 us (6%)
    pallas_call x2, Pallas kernels, exchange(): pl.pallas_call(lambda *refs: exchange_kernel(rows, cols, last, scans, *re...  79.4 us
    pallas_call x2, Pallas kernels, step(): pl.pallas_call(step_kernel, out_shape=(jax.ShapeDtypeStruct((2, full, ful...  19.4 us
    pallas_call x1, Pallas kernels, halo(): pl.pallas_call(lambda *refs: halo_kernel(rows, cols, *refs), out_shape=(j...  10.4 us
    unnamed x15, local copies, waits for them, and re-layouts  3.31 us

profile of v5, /device:TPU:0, one launch (start us, length us, event | category | flops | bytes accessed | tf_op | source)
XLA Modules:
  0.0 116.6 jit_solution(7649312771194676313)
XLA Ops:
  0.6 0.0 copy-start.6
  0.6 0.0 copy-start.5
  0.7 0.0 copy-start.4
  0.7 0.0 copy-start.2
  0.7 0.0 copy-start.3
  0.7 0.9 broadcast_in_dim.7
  1.6 0.1 broadcast_in_dim.8.refs_1_
  1.6 1.3 %copy.8 = f32[4,32,8,2,128]{4,2,0,1,3:T(8,128)S(1)} copy(f32[4,32,8,2,128]{4,2,3,1,0:T(8,128)} %bitcast.17) | data formatting | bytes 2097152 | tf_op jit(solution)/shard_map/reshape | solution.py:564
  3.0 0.0 copy-done.2
  3.0 10.4 %shard_map.77 = (f32[2,384,384]{2,1,0:T(8,128)S(1)}, s32[3,3,4,128]{3,2,1,0:T(4,128)S(1)}) custom-call(f32[2,128,128]{2,1,0:T(8,128)S(1)} %copy-done.2, s32[4,128]{1,0:T(4,128)S(1)} %broadcast_in_dim.8.refs_1_), custom_call_target="tpu_custom_call" | custom-call | tf_op jit(solution)/shard_map/pallas_call | solution.py:177
  13.5 0.0 copy-done.6
  13.5 0.0 copy-done.5
  13.5 0.0 copy-done.4
  13.5 0.0 copy-done.3
  13.5 9.7 %shard_map.78 = (f32[2,384,384]{2,1,0:T(8,128)S(1)}, f32[64,5,8,128]{3,2,1,0:T(8,128)}) custom-call(s32[2,2]{1,0:T(2,128)S(1)} %bitcast.15, f32[2,384,384]{2,1,0:T(8,128)S(1)} %get-tuple-element.14.obj, f32[64,4,8,128]{3,2,1,0:T(8,128)S(1)} %bitcast.10, f32[2,256,256]{2,1,0:T(8,128)S(1)} %bitcast.13, bf16[8,256,256]{2,1,0:T(8,128)(2,1)S(1)} %copy-done.5, ...), custom_call_target="tpu_custom_call" | custom-call | flops 3221225472 | bytes 6291456 | tf_op jit(solution)/shard_map/pallas_call | solution.py:539
  23.2 0.0 copy-start.1
  23.2 1.3 %copy-done.1 = f32[64,5,8,128]{3,2,1,0:T(8,128)S(1)} copy-done((f32[64,5,8,128]{3,2,1,0:T(8,128)S(1)}, f32[64,5,8,128]{3,2,1,0:T(8,128)}, u32[]{:S(2)}) %copy-start.1) | copy-done | bytes 1310744
  24.5 47.4 %shard_map.79 = (f32[2,128,128]{2,1,0:T(8,128)S(1)}, f32[64,4,8,128]{3,2,1,0:T(8,128)S(1)}, f32[2,384,384]{2,1,0:T(8,128)S(1)}) custom-call(f32[2,128,128]{2,1,0:T(8,128)S(1)} %copy-done.2, f32[64,4,8,128]{3,2,1,0:T(8,128)S(1)} %bitcast.11, s32[3,3,4,128]{3,2,1,0:T(4,128)S(1)} %get-tuple-element.13.refs_2_, f32[2,384,384]{2,1,0:T(8,128)S(1)} %get-tuple-element.15.refs_3_, ...), custom_call_target="tpu_custom_call" | custom-call | tf_op jit(solution)/shard_map/pallas_call | solution.py:381
  71.9 9.7 %shard_map.80 = (f32[2,384,384]{2,1,0:T(8,128)S(1)}, f32[64,5,8,128]{3,2,1,0:T(8,128)}) custom-call(s32[2,2]{1,0:T(2,128)S(1)} %bitcast.16, f32[2,384,384]{2,1,0:T(8,128)S(1)} %get-tuple-element.19.obj, f32[64,4,8,128]{3,2,1,0:T(8,128)S(1)} %get-tuple-element.18.tiles.refs_1_, f32[2,256,256]{2,1,0:T(8,128)S(1)} %bitcast.14, ...), custom_call_target="tpu_custom_call" | custom-call | flops 3221225472 | bytes 6291456 | tf_op jit(solution)/shard_map/pallas_call | solution.py:539
  81.6 0.0 copy-start
  81.6 1.3 %copy-done = f32[64,5,8,128]{3,2,1,0:T(8,128)S(1)} copy-done((f32[64,5,8,128]{3,2,1,0:T(8,128)S(1)}, f32[64,5,8,128]{3,2,1,0:T(8,128)}, u32[]{:S(2)}) %copy-start) | copy-done | bytes 1310744
  82.9 32.0 %shard_map.81 = (f32[2,128,128]{2,1,0:T(8,128)S(1)}, f32[64,4,8,128]{3,2,1,0:T(8,128)S(1)}) custom-call(f32[2,128,128]{2,1,0:T(8,128)S(1)} %get-tuple-element.17.refs_0_, f32[64,4,8,128]{3,2,1,0:T(8,128)S(1)} %get-tuple-element.18.tiles.refs_1_, s32[3,3,4,128]{3,2,1,0:T(4,128)S(1)} %get-tuple-element.13.refs_2_, ...), custom_call_target="tpu_custom_call" | custom-call | tf_op jit(solution)/shard_map/pallas_call | solution.py:381
  114.9 1.1 copy.9
  116.0 0.7 copy.11
Async XLA Ops:
  0.6 12.8 %copy-start.6 = (bf16[2,256,256]{2,1,0:T(8,128)(2,1)S(1)}, bf16[2,256,256]{2,1,0:T(8,128)(2,1)}, u32[]{:S(2)}) copy-start(bf16[2,256,256]{2,1,0:T(8,128)(2,1)} %constant.5.clone.order) | copy-start | bytes 786436
  0.6 12.8 %copy-start.5 = (bf16[8,256,256]{2,1,0:T(8,128)(2,1)S(1)}, bf16[8,256,256]{2,1,0:T(8,128)(2,1)}, u32[]{:S(2)}) copy-start(bf16[8,256,256]{2,1,0:T(8,128)(2,1)} %constant.4.clone.tab) | copy-start | bytes 3145732
  0.7 12.8 %copy-start.4 = (s32[1,1,2,2]{3,2,1,0:T(2,128)S(1)}, s32[1,1,2,2]{3,2,1,0:T(2,128)}, u32[]{:S(2)}) copy-start(s32[1,1,2,2]{3,2,1,0:T(2,128)} %param.9) | copy-start | bytes 52
  0.7 2.3 %copy-start.2 = (f32[2,128,128]{2,1,0:T(8,128)S(1)}, f32[2,128,128]{2,1,0:T(8,128)}, u32[]{:S(2)}) copy-start(f32[2,128,128]{2,1,0:T(8,128)} %refs_0_.3) | copy-start | bytes 393220
  0.7 12.8 %copy-start.3 = (f32[1,1,2,256,256]{4,3,2,1,0:T(8,128)S(1)}, f32[1,1,2,256,256]{4,3,2,1,0:T(8,128)}, u32[]{:S(2)}) copy-start(f32[1,1,2,256,256]{4,3,2,1,0:T(8,128)} %param.8) | copy-start | bytes 1572868
  23.2 1.3 %copy-start.1 = (f32[64,5,8,128]{3,2,1,0:T(8,128)S(1)}, f32[64,5,8,128]{3,2,1,0:T(8,128)}, u32[]{:S(2)}) copy-start(f32[64,5,8,128]{3,2,1,0:T(8,128)} %get-tuple-element.16.refs_4_) | copy-start | bytes 3932164
  81.6 1.3 %copy-start = (f32[64,5,8,128]{3,2,1,0:T(8,128)S(1)}, f32[64,5,8,128]{3,2,1,0:T(8,128)}, u32[]{:S(2)}) copy-start(f32[64,5,8,128]{3,2,1,0:T(8,128)} %get-tuple-element.21.refs_4_) | copy-start | bytes 3932164
